TPU v7x, 512 devices: a whole 4x8x8 slice. The times are simulated.
512 devices in a mesh: section: 4 (over z_hi), seq: 32 (over x, y), head: 4 (over z_lo, core).
Axes of the slice: x: 4, y: 8, z: 8 (z_hi: 4, z_lo: 2; z = z_hi * 2 + z_lo), core: 2. Of those that a mesh axis runs over, the one named last changes fastest.
Arguments:
- lengths: int32 [4], replicated, may hold values from 1 to 3072, 4096 in all
- adapter: int32 [4], replicated, may hold values from 0 to 7
- query: bfloat16 [4, 4096, 1536], P('section', 'seq', 'head'), may hold values from -120 to 120
- previous_keys: bfloat16 [4, 4096, 1536], P('section', 'seq', 'head'), may hold values from -6 to 6
- previous_values: bfloat16 [4, 4096, 1536], P('section', 'seq', 'head'), may hold values from -6 to 6
- stream: bfloat16 [4, 4096, 3072], P('section', 'seq', 'head'), may hold values from -6 to 6
- gate: float32 [4, 4, 3072], P('section', None, 'head'), may hold values from 0.5 to 1.5
- output_matrix: bfloat16 [4, 1536, 3072], P('section', 'head'), may hold values from -0.15625 to 0.15625
- adapter_down: bfloat16 [4, 8, 1536, 64], P('section', None, 'head'), may hold values from -0.15625 to 0.15625
- adapter_up: bfloat16 [4, 8, 64, 3072], P('section', None, None, 'head'), may hold values from -0.75 to 0.75
Outputs:
- block_out: bfloat16 [4, 4096, 3072], P('section', 'seq', 'head')
Inputs may be any that keep to these rules, and one draw needn't show every extreme that they name: `lengths`: the 4 counts fill all 4096 tokens in order; the largest is exactly 3072.
All inputs are finite; a program needn't handle non-finite values.
Results may differ from a plain program's by a relative error of at most 0.0075.
Values may be sent and summed in bfloat16 or wider, within the bound.
No kernel may reach another device: no remote copies, remote signals or barrier semaphores. Data moves between devices by JAX's collectives and lax.ppermute only.
A program may use at most 64 MiB of HBM per device.

v0:
```python
import math

import jax
import jax.numpy as jnp
from jax import lax
from jax.sharding import PartitionSpec as P

HEAD_SIZE = 128


NEG_FILL = -1e30


def from_behind(block, axis, distance):
    devices = range(lax.axis_size(axis))
    route = [((i - distance) % len(devices), i) for i in devices]
    return lax.ppermute(block, axis, route)


def segment_of(position, request_ends):
    hits = (position[:, None] >= request_ends[None, :]).astype(jnp.int32)
    return jnp.sum(hits, axis=1)


def shards(
    lengths,
    adapter,
    query,
    previous_keys,
    previous_values,
    stream,
    gate,
    output_matrix,
    adapter_down,
    adapter_up,
):
    token_rows = query.shape[1]
    feat_width = query.shape[2]
    heads_here = feat_width // HEAD_SIZE
    req_count = lengths.shape[0]
    score_scale = 1.0 / math.sqrt(HEAD_SIZE)
    request_ends = jnp.cumsum(lengths)
    position = lax.axis_index("seq") * token_rows + jnp.arange(token_rows, dtype=jnp.int32)
    query_seg = segment_of(position, request_ends)
    request_member = (query_seg[:, None] == jnp.arange(req_count, dtype=jnp.int32)[None, :]).astype(
        jnp.float32
    )
    received_state = from_behind(stream, "section", 1)
    queries = query[0].reshape(token_rows, heads_here, HEAD_SIZE)
    start_state = (
        jnp.full((token_rows, heads_here), NEG_FILL, jnp.float32),
        jnp.zeros((token_rows, heads_here), jnp.float32),
        jnp.zeros((token_rows, heads_here, HEAD_SIZE), jnp.float32),
    )
    keys = lax.all_gather(previous_keys, "seq", axis=1, tiled=True)
    values = lax.all_gather(previous_values, "seq", axis=1, tiled=True)
    piece_len = keys.shape[1]
    block_len = math.gcd(piece_len, 1024)
    block_count = piece_len // block_len
    key_blocks = keys[0].reshape(block_count, block_len, heads_here, HEAD_SIZE)
    value_blocks = values[0].reshape(block_count, block_len, heads_here, HEAD_SIZE)
    key_pos = jnp.arange(piece_len, dtype=jnp.int32).reshape(block_count, block_len)

    def advance(state_in, block_item):
        key_rows, value_rows, key_place = block_item
        key_seg = segment_of(key_place, request_ends)
        allowed = query_seg[:, None] == key_seg[None, :]
        run_max, run_sum, run_acc = state_in
        scores = (
            jnp.einsum("qhd,khd->qhk", queries, key_rows, preferred_element_type=jnp.float32)
            * score_scale
        )
        scores = jnp.where(allowed[:, None, :], scores, NEG_FILL)
        new_max = jnp.maximum(run_max, jnp.max(scores, axis=2))
        factor = jnp.exp(run_max - new_max)
        weights = jnp.exp(scores - new_max[:, :, None])
        new_sum = run_sum * factor + jnp.sum(weights, axis=2)
        weights_bf = weights.astype(jnp.bfloat16)
        new_acc = run_acc * factor[:, :, None] + jnp.einsum(
            "qhk,khd->qhd", weights_bf, value_rows, preferred_element_type=jnp.float32
        )
        state_out = (new_max, new_sum, new_acc)
        return (state_out, None)

    state_end, unused = lax.scan(advance, start_state, (key_blocks, value_blocks, key_pos))
    run_max, run_sum, run_acc = state_end
    attn = (run_acc / run_sum[:, :, None]).reshape(token_rows, feat_width).astype(jnp.bfloat16)
    rank_middle = jnp.zeros((token_rows, adapter_down.shape[3]), jnp.float32)
    for request_index in range(req_count):
        down_factor = lax.dynamic_index_in_dim(
            adapter_down[0], adapter[request_index], 0, keepdims=False
        )
        rank_middle = rank_middle + request_member[:, request_index : request_index + 1] * jnp.dot(
            attn, down_factor, preferred_element_type=jnp.float32
        )
    rank_middle = lax.psum(rank_middle.astype(jnp.bfloat16), "head")
    adapter_term = jnp.zeros((token_rows, adapter_up.shape[3]), jnp.float32)
    for request_index in range(req_count):
        up_factor = lax.dynamic_index_in_dim(
            adapter_up[0], adapter[request_index], 0, keepdims=False
        )
        adapter_term = adapter_term + request_member[
            :, request_index : request_index + 1
        ] * jnp.dot(rank_middle, up_factor, preferred_element_type=jnp.float32)
    partial_value = jnp.dot(attn, output_matrix[0], preferred_element_type=jnp.float32)
    projected_rows = lax.psum_scatter(
        partial_value.astype(jnp.bfloat16), "head", scatter_dimension=1, tiled=True
    ).astype(jnp.float32)
    gate_values = jnp.dot(request_member, gate[0], precision=lax.Precision.HIGHEST)
    final_output = received_state[0].astype(jnp.float32) + gate_values * (
        projected_rows + adapter_term
    )
    return final_output.astype(jnp.bfloat16)[None]


def solution(mesh):
    placed = (
        P(),
        P(),
        P("section", "seq", "head"),
        P("section", "seq", "head"),
        P("section", "seq", "head"),
        P("section", "seq", "head"),
        P("section", None, "head"),
        P("section", "head", None),
        P("section", None, "head", None),
        P("section", None, None, "head"),
    )
    return jax.shard_map(
        shards, mesh=mesh, in_specs=placed, out_specs=P("section", "seq", "head"), check_vma=False
    )
```

profile of v0, /device:TPU:1, one launch (start us, length us, event | category | flops | bytes accessed | tf_op | source)
XLA Modules:
  0.0 261.0 jit_solution(1460724235786589874)
XLA Ops:
  8.1 6.6 %collective-permute-start = (bf16[1,128,768]{2,1,0:T(8,128)(2,1)}, bf16[1,128,768]{2,1,0:T(8,128)(2,1)}, u32[]{:S(2)}, u32[]{:S(2)}) collective-permute-start(bf16[1,128,768]{2,1,0:T(8,128)(2,1)} %param.17), channel_id=1, source_target_pairs={{384,0},{0,128},{128,256},{256,384},{385,1},{1,129},{129,257},{257... | collective-permute-start | bytes 589832 | tf_op jit(solution)/shard_map/ppermute | solution.py:17
  27.0 70.6 %all-gather.3.cloned.1.call-done = bf16[1,4096,384]{2,1,0:T(8,128)(2,1)} async-done(((bf16[1,128,384]{2,1,0:T(8,128)(2,1)}), bf16[1,4096,384]{2,1,0:T(8,128)(2,1)}) %all-gather.3.cloned.1.call-update) | async-done | bytes 3145744 | tf_op jit(solution)/shard_map/all_gather | solution.py:55
  97.6 9.0 %reshape.94 = bf16[4,1024,3,128]{3,2,1,0:T(4,128)(2,1)} reshape(bf16[1,4096,384]{2,1,0:T(8,128)(2,1)} %all-gather.3.cloned.1.call-done) | data formatting | bytes 6291456 | tf_op jit(solution)/shard_map/reshape;squeeze | solution.py:60
  106.6 4.6 %copy.23 = bf16[4,1024,3,128]{3,1,2,0:T(8,128)(2,1)} copy(bf16[4,1024,3,128]{3,2,1,0:T(4,128)(2,1)} %reshape.94) | data formatting | bytes 6291456
  111.2 71.7 %all-gather.5.cloned.1.call-done = bf16[1,4096,384]{2,1,0:T(8,128)(2,1)} async-done(((bf16[1,128,384]{2,1,0:T(8,128)(2,1)}), bf16[1,4096,384]{2,1,0:T(8,128)(2,1)}) %all-gather.5.cloned.1.call-update) | async-done | bytes 3145744 | tf_op jit(solution)/shard_map/all_gather | solution.py:56
  182.9 9.0 %reshape.95 = bf16[4,1024,3,128]{3,2,1,0:T(4,128)(2,1)} reshape(bf16[1,4096,384]{2,1,0:T(8,128)(2,1)} %all-gather.5.cloned.1.call-done) | data formatting | bytes 6291456 | tf_op jit(solution)/shard_map/reshape;squeeze | solution.py:61
  191.9 7.2 %copy.25 = bf16[4,1024,3,128]{1,3,2,0:T(8,128)(2,1)} copy(bf16[4,1024,3,128]{3,2,1,0:T(4,128)(2,1)} %reshape.95) | data formatting | bytes 6291456
  199.1 25.9 %while.15 = (s32[]{:T(128)}, f32[128,3]{0,1:T(4,128)S(1)}, f32[128,3]{0,1:T(4,128)S(1)}, f32[128,3,128]{0,2,1:T(8,128)S(1)}, s32[128]{0:T(128)S(1)}, /*index=5*/...) while((s32[]{:T(128)}, f32[128,3]{0,1:T(4,128)S(1)}, ...), condition=%wide.region_6.7_spmd.clone, body=%wide.region_2.6_spmd.clone.sunk | while | flops 204370816 | bytes 13383345 | solution.py:85
  199.4 2.7 %fusion.74 = (f32[128,3]{0,1:T(4,128)S(1)}, f32[128,3,1024]{0,2,1:T(8,128)}) fusion(bf16[128,3,128]{2,0,1:T(8,128)(2,1)S(1)} %get-tuple-element.246, bf16[4,1024,3,128]{3,1,2,0:T(8,128)(2,1)} %get-tuple-element.245, s32[]{:T(128)} %get-tuple-element.226, pred[128,1024]{0,1:T(8,128)(4,1)S(1)} %broadcast_compare_fusion.2), kind=kOutput, calls=%fused_computation.80.clone.1 | convolution fusion | flops 101842560 | bytes 2590720 | tf_op jit(solution)/shard_map/while/body/eval_jaxpr/qhd,khd->qhk/dot_general | solution.py:70
  202.1 1.8 fusion.75
  204.0 1.5 fusion.77
  205.9 2.7 %fusion.74 = (f32[128,3]{0,1:T(4,128)S(1)}, f32[128,3,1024]{0,2,1:T(8,128)}) fusion(bf16[128,3,128]{2,0,1:T(8,128)(2,1)S(1)} %get-tuple-element.246, bf16[4,1024,3,128]{3,1,2,0:T(8,128)(2,1)} %get-tuple-element.245, s32[]{:T(128)} %get-tuple-element.226, pred[128,1024]{0,1:T(8,128)(4,1)S(1)} %broadcast_compare_fusion.2), kind=kOutput, calls=%fused_computation.80.clone.1 | convolution fusion | flops 101842560 | bytes 2590720 | tf_op jit(solution)/shard_map/while/body/eval_jaxpr/qhd,khd->qhk/dot_general | solution.py:70
  208.6 1.8 fusion.75
  210.5 1.5 fusion.77
  212.4 2.7 %fusion.74 = (f32[128,3]{0,1:T(4,128)S(1)}, f32[128,3,1024]{0,2,1:T(8,128)}) fusion(bf16[128,3,128]{2,0,1:T(8,128)(2,1)S(1)} %get-tuple-element.246, bf16[4,1024,3,128]{3,1,2,0:T(8,128)(2,1)} %get-tuple-element.245, s32[]{:T(128)} %get-tuple-element.226, pred[128,1024]{0,1:T(8,128)(4,1)S(1)} %broadcast_compare_fusion.2), kind=kOutput, calls=%fused_computation.80.clone.1 | convolution fusion | flops 101842560 | bytes 2590720 | tf_op jit(solution)/shard_map/while/body/eval_jaxpr/qhd,khd->qhk/dot_general | solution.py:70
  215.1 1.8 fusion.75
  217.0 1.5 fusion.77
  218.8 2.7 %fusion.74 = (f32[128,3]{0,1:T(4,128)S(1)}, f32[128,3,1024]{0,2,1:T(8,128)}) fusion(bf16[128,3,128]{2,0,1:T(8,128)(2,1)S(1)} %get-tuple-element.246, bf16[4,1024,3,128]{3,1,2,0:T(8,128)(2,1)} %get-tuple-element.245, s32[]{:T(128)} %get-tuple-element.226, pred[128,1024]{0,1:T(8,128)(4,1)S(1)} %broadcast_compare_fusion.2), kind=kOutput, calls=%fused_computation.80.clone.1 | convolution fusion | flops 101842560 | bytes 2590720 | tf_op jit(solution)/shard_map/while/body/eval_jaxpr/qhd,khd->qhk/dot_general | solution.py:70
  221.6 1.8 fusion.75
  223.4 1.5 fusion.77
  225.1 1.5 convolution_convert_fusion
  227.2 13.3 %psum.7 = bf16[128,64]{0,1:T(8,128)(2,1)S(1)} all-reduce(bf16[128,64]{0,1:T(8,128)(2,1)S(1)} %fusion.21), channel_id=1, replica_groups=mesh['section'=4,'seq'=32,'head'=4] {'head'}, use_global_device_ids=true, to_apply=%region_8.9 | all-reduce | flops 8192 | bytes 32768 | tf_op jit(solution)/shard_map/psum | solution.py:96
  244.0 8.4 %reduce-scatter.2.cloned.1.call-done = bf16[128,768]{1,0:T(8,128)(2,1)} async-done(((bf16[128,3072]{1,0:T(8,128)(2,1)}), bf16[128,768]{1,0:T(8,128)(2,1)}) %reduce-scatter.2.cloned.1.call-update) | async-done | bytes 196624 | tf_op jit(solution)/shard_map/reduce_scatter | solution.py:106
  252.4 2.0 fusion.23
  (64 shorter events, 11.9 us)
Async XLA Ops:
  6.5 218.5 %copy-start = (bf16[1,384,3072]{2,1,0:T(8,128)(2,1)S(1)}, bf16[1,384,3072]{2,1,0:T(8,128)(2,1)}, u32[]{:S(2)}) copy-start(bf16[1,384,3072]{2,1,0:T(8,128)(2,1)} %param.19) | copy-start | bytes 7077892
  6.5 91.1 %all-gather.3.cloned.1.call-start = ((), (), s32[]{:S(2)}) async-start(), calls=%async_computation.1 | async-start | bytes 3244032 | tf_op jit(solution)/shard_map/all_gather | solution.py:55
  7.3 175.6 %all-gather.5.cloned.1.call-start = ((), (), s32[]{:S(2)}) async-start(), calls=%async_computation.2 | async-start | bytes 3244032 | tf_op jit(solution)/shard_map/all_gather | solution.py:56
  8.0 244.4 %reduce-scatter.2.cloned.1.call-start = ((), (), s32[]{:S(2)}) async-start(), calls=%async_computation.3 | async-start | bytes 983040 | tf_op jit(solution)/shard_map/reduce_scatter | solution.py:106
  8.1 235.9 %collective-permute-start = (bf16[1,128,768]{2,1,0:T(8,128)(2,1)}, bf16[1,128,768]{2,1,0:T(8,128)(2,1)}, u32[]{:S(2)}, u32[]{:S(2)}) collective-permute-start(bf16[1,128,768]{2,1,0:T(8,128)(2,1)} %param.17), channel_id=1, source_target_pairs={{384,0},{0,128},{128,256},{256,384},{385,1},{1,129},{129,257},{257... | collective-permute-start | bytes 589832 | tf_op jit(solution)/shard_map/ppermute | solution.py:17
  202.1 1.9 copy-start.1
  208.6 1.9 copy-start.1
  215.1 1.9 copy-start.1
  221.6 1.9 copy-start.1
  225.1 1.5 copy-start.2
Sparse Core Ops, SparseCore 0:
  10.5 87.0 all-gather.2
  100.8 82.0 all-gather.4
  226.7 25.6 reduce-scatter.1
where the time goes:
time: 262 us; the launch traced here: 261 us
  waiting for transfers between devices  152 us (58%)
  local copies, waits for them, and re-layouts  32.9 us (13%)
  matrix products  25.6 us (10%)
  between operations  20.8 us (8%)
  blocking collectives  13.3 us (5%)
  other arithmetic  9.19 us (4%)
  starting transfers between devices  6.72 us (3%)
    all_gather x1, waiting for transfers between devices, shards(): values = lax.all_gather(previous_values, 'seq', axis=1, tiled=True)  71.7 us
    all_gather x1, waiting for transfers between devices, shards(): keys = lax.all_gather(previous_keys, 'seq', axis=1, tiled=True)  70.6 us
    psum x1, blocking collectives, shards(): rank_middle = lax.psum(rank_middle.astype(jnp.bfloat16), 'head')  13.3 us
    unnamed x8, local copies, waits for them, and re-layouts  12.9 us
    dot_general x4, matrix products, advance(): jnp.einsum('qhd,khd->qhk', queries, key_rows, preferred_element_type=jnp....  10.8 us
    another operation x1, local copies, waits for them, and re-layouts, shards(): key_blocks = keys[0].reshape(block_count, block_len, heads_here, HEAD_SIZE)  9.01 us
    another operation x1, local copies, waits for them, and re-layouts, shards(): values[0].reshape(block_count, block_len, heads_here, HEAD_SIZE)  9.01 us
    reduce_scatter x1, waiting for transfers between devices, shards(): lax.psum_scatter(partial_value.astype(jnp.bfloat16), 'head', scatter_dime...  8.42 us
  transfers between devices with their start and end apart: 4, of which 3 were waited for; matrix products, arithmetic and copies ran while one was open for 25% of the time, Pallas kernels for 0%

commit v1 on v0

v1 whole, which is shorter than its diff:
```python
import functools
import math

import jax
import jax.numpy as jnp
from jax import lax
from jax.experimental import pallas as pl
from jax.experimental.pallas import tpu as pltpu
from jax.sharding import Mesh, PartitionSpec as P

HEAD = 128
NEG = -1e30
NX, NYH, NYL = 4, 4, 2
NZ, NC = 2, 2
STAT_ROWS = 16
F32 = jnp.float32
BF16 = jnp.bfloat16
VMEM_LIMIT = 48 * 1024 * 1024


def segment_of(position, info_ref, reqs):
    seg = jnp.zeros(position.shape, jnp.int32)
    for r in range(reqs):
        seg = seg + (position >= info_ref[r]).astype(jnp.int32)
    return seg


def attend_kernel(reqs, info_ref, q_ref, kv_ref, out_ref, kx_ref, vt_ref):
    rows = q_ref.shape[1]
    feats = q_ref.shape[2]
    heads = feats // HEAD
    keys = kv_ref.shape[0]
    step = pl.program_id(0)
    my_x, my_yh, my_yl = info_ref[reqs], info_ref[reqs + 1], info_ref[reqs + 2]
    scale = math.log2(math.e) / math.sqrt(HEAD)

    @pl.when(step == 0)
    def prepare():
        row = lax.broadcasted_iota(jnp.int32, (keys, HEAD), 0)
        lane = lax.broadcasted_iota(jnp.int32, (keys, HEAD), 1)
        block = row // rows
        place = ((my_x * NYH + block) * NYL + my_yl) * rows + (row - block * rows)
        seg = segment_of(place, info_ref, reqs)
        bar = jnp.where((lane < reqs) & (lane != seg), NEG, 0.0).astype(BF16)
        for h in range(heads):
            kx_ref[h, :, 0:HEAD] = kv_ref[:, h * HEAD : (h + 1) * HEAD]
            kx_ref[h, :, HEAD : 2 * HEAD] = bar
        vt_ref[...] = kv_ref[:, feats : 2 * feats].T

    n_q = NYL * rows
    first = (step * NYH + my_yh) * n_q
    place = first + lax.broadcasted_iota(jnp.int32, (n_q, HEAD), 0)
    lane = lax.broadcasted_iota(jnp.int32, (n_q, HEAD), 1)
    member = (segment_of(place, info_ref, reqs) == lane).astype(F32).astype(BF16)
    high, mid, low = [], [], []
    for h in range(heads):
        queries = q_ref[:, :, h * HEAD : (h + 1) * HEAD].reshape(n_q, HEAD)
        queries = jnp.concatenate([queries, member], axis=1)
        scores = lax.dot_general(kx_ref[h], queries, (((1,), (1,)), ((), ())), preferred_element_type=F32)
        top = jnp.max(scores, axis=0, keepdims=True)
        weights = jnp.exp2((scores - top) * scale)
        total = jnp.sum(weights, axis=0, keepdims=True)
        part = jnp.dot(vt_ref[h * HEAD : (h + 1) * HEAD, :], weights.astype(BF16), preferred_element_type=F32)
        part = (part * (1.0 / total)).astype(BF16)
        for i in range(NYL):
            out_ref[i, h * HEAD : (h + 1) * HEAD, :] = part[:, i * rows : (i + 1) * rows]
        level = top * scale + jnp.log2(total)
        a = level.astype(BF16).astype(F32)
        b = (level - a).astype(BF16).astype(F32)
        high.append(a)
        mid.append(b)
        low.append(level - a - b)
    blank = [jnp.zeros((1, n_q), F32)] * (STAT_ROWS - 3 * heads)
    stats = jnp.concatenate(high + mid + low + blank, axis=0).astype(BF16)
    for i in range(NYL):
        out_ref[i, feats : feats + STAT_ROWS, :] = stats[:, i * rows : (i + 1) * rows]


def project_kernel(reqs, info_ref, part_ref, down_ref, w_ref, send_ref, keep_ref):
    groups = part_ref.shape[0]
    feats, out_feats = w_ref.shape
    rows = part_ref.shape[2]
    heads = feats // HEAD
    quarter = out_feats // (NZ * NC)
    stat = part_ref[:, feats : feats + STAT_ROWS, :].astype(F32)
    level = stat[:, 0:heads] + stat[:, heads : 2 * heads] + stat[:, 2 * heads : 3 * heads]
    share = jnp.exp2(level - jnp.max(level, axis=0, keepdims=True))
    share = share / jnp.sum(share, axis=0, keepdims=True)
    columns = []
    for h in range(heads):
        acc = jnp.zeros((HEAD, rows), F32)
        for g in range(groups):
            acc = acc + part_ref[g, h * HEAD : (h + 1) * HEAD, :].astype(F32) * share[g, h : h + 1, :]
        columns.append(acc.T.astype(BF16))
    attn = jnp.concatenate(columns, axis=1)

    place = info_ref[2 * reqs] + lax.broadcasted_iota(jnp.int32, (rows, 1), 0)
    seg = segment_of(place, info_ref, reqs)
    rank = jnp.zeros((rows, down_ref.shape[2]), F32)
    for r in range(reqs):
        mid = jnp.dot(attn, down_ref[info_ref[reqs + r]], preferred_element_type=F32)
        rank = rank + jnp.where(seg == r, mid, 0.0)
    rank = jnp.concatenate([rank, jnp.zeros((rows, HEAD - rank.shape[1]), F32)], axis=1)
    core = info_ref[2 * reqs + 1]
    for z in range(NZ):
        for ref, c in ((send_ref, 1 - core), (keep_ref, core)):
            start = pl.multiple_of((z * NC + c) * quarter, quarter)
            product = jnp.dot(attn, w_ref[:, pl.ds(start, quarter)], preferred_element_type=F32)
            ref[:, z * quarter : (z + 1) * quarter] = product.astype(ref.dtype)
    send_ref[:, NZ * quarter : NZ * quarter + HEAD] = rank.astype(send_ref.dtype)
    keep_ref[:, NZ * quarter : NZ * quarter + HEAD] = rank.astype(keep_ref.dtype)


def finish_kernel(reqs, info_ref, mine_ref, other_ref, state_ref, gate_ref, up_ref, out_ref):
    rows, quarter = out_ref.shape
    ranks = up_ref.shape[1]
    place = info_ref[2 * reqs] + lax.broadcasted_iota(jnp.int32, (rows, 1), 0)
    seg = segment_of(place, info_ref, reqs)
    rank = mine_ref[:, quarter : quarter + ranks] + other_ref[:, quarter : quarter + ranks].astype(F32)
    rank = rank.astype(BF16)
    branch = mine_ref[:, 0:quarter] + other_ref[:, 0:quarter].astype(F32)
    gates = jnp.zeros((rows, quarter), F32)
    for r in range(reqs):
        chosen = jnp.where(seg == r, rank.astype(F32), 0.0).astype(BF16)
        branch = branch + jnp.dot(chosen, up_ref[info_ref[reqs + r]], preferred_element_type=F32)
        gates = jnp.where(seg == r, gate_ref[r : r + 1, :], gates)
    out_ref[...] = (state_ref[...].astype(F32) + gates * branch).astype(out_ref.dtype)


def shards(lengths, adapter, query, previous_keys, previous_values, stream, gate, output_matrix, adapter_down, adapter_up):
    rows, feats = query.shape[1:]
    reqs = lengths.shape[0]
    out_feats = output_matrix.shape[2]
    quarter = out_feats // (NZ * NC)
    group = NX * NYL
    my_x, my_yh, my_yl = lax.axis_index("x"), lax.axis_index("yh"), lax.axis_index("yl")
    my_z, my_core = lax.axis_index("zl"), lax.axis_index("core")
    ends = jnp.cumsum(lengths).astype(jnp.int32)
    first = ((my_x * NYH + my_yh) * NYL + my_yl) * rows
    info_attend = jnp.concatenate([ends, jnp.stack([my_x, my_yh, my_yl]).astype(jnp.int32)])
    info = jnp.concatenate([ends, adapter, jnp.stack([first, my_core]).astype(jnp.int32)])
    smem = pl.BlockSpec(memory_space=pltpu.SMEM)
    vmem = pl.BlockSpec(memory_space=pltpu.VMEM)
    params = pltpu.CompilerParams(vmem_limit_bytes=VMEM_LIMIT)

    sections = lax.axis_size("section")
    state = lax.ppermute(stream[0], "section", [(i, (i + 1) % sections) for i in range(sections)])

    queries = lax.all_to_all(jnp.broadcast_to(query, (group, rows, feats)), ("x", "yl"), 0, 0, tiled=True)
    kv = jnp.concatenate([previous_keys[0], previous_values[0]], axis=1)
    kv = lax.all_gather(kv, "yh", axis=0, tiled=True)

    keys = NYH * rows
    parts = pl.pallas_call(
        functools.partial(attend_kernel, reqs),
        grid=(NX,),
        in_specs=[
            smem,
            pl.BlockSpec((NYL, rows, feats), lambda i: (i, 0, 0)),
            pl.BlockSpec((keys, 2 * feats), lambda i: (0, 0)),
        ],
        out_specs=pl.BlockSpec((NYL, feats + STAT_ROWS, rows), lambda i: (i, 0, 0)),
        out_shape=jax.ShapeDtypeStruct((group, feats + STAT_ROWS, rows), BF16),
        scratch_shapes=[pltpu.VMEM((feats // HEAD, keys, 2 * HEAD), BF16), pltpu.VMEM((feats, keys), BF16)],
        compiler_params=params,
    )(info_attend, queries, kv)

    parts = lax.all_to_all(parts, ("x", "yl"), 0, 0, tiled=True)

    width = NZ * quarter + HEAD
    send, keep = pl.pallas_call(
        functools.partial(project_kernel, reqs),
        in_specs=[smem, vmem, vmem, vmem],
        out_specs=[vmem, vmem],
        out_shape=[jax.ShapeDtypeStruct((rows, width), BF16), jax.ShapeDtypeStruct((rows, width), F32)],
        compiler_params=params,
    )(info, parts, adapter_down[0], output_matrix[0])

    chip = keep + lax.ppermute(send, "core", [(0, 1), (1, 0)]).astype(F32)
    rank = chip[:, NZ * quarter :]
    here = lax.dynamic_slice_in_dim(chip, my_z * quarter, quarter, 1)
    there = lax.dynamic_slice_in_dim(chip, (1 - my_z) * quarter, quarter, 1)
    mine = jnp.concatenate([here, rank], axis=1)
    other = jnp.concatenate([there, rank], axis=1).astype(BF16)
    other = lax.ppermute(other, "zl", [(0, 1), (1, 0)])

    out = pl.pallas_call(
        functools.partial(finish_kernel, reqs),
        in_specs=[smem] + [vmem] * 5,
        out_specs=vmem,
        out_shape=jax.ShapeDtypeStruct((rows, quarter), BF16),
        compiler_params=params,
    )(info, mine, other, state, gate[0], adapter_up[0])
    return out[None]


def solution(mesh):
    devices = mesh.devices.reshape(mesh.shape["section"], NX, NYH, NYL, NZ, NC)
    fine = Mesh(devices, ("section", "x", "yh", "yl", "zl", "core"))
    seq, head = ("x", "yh", "yl"), ("zl", "core")
    placed = (
        P(),
        P(),
        P("section", seq, head),
        P("section", seq, head),
        P("section", seq, head),
        P("section", seq, head),
        P("section", None, head),
        P("section", head, None),
        P("section", None, head, None),
        P("section", None, None, head),
    )
    return jax.shard_map(shards, mesh=fine, in_specs=placed, out_specs=P("section", seq, head), check_vma=False)
```

time: 262 us -> 85.5 us (0.33)
  the two profiles are of different devices: /device:TPU:1 before, /device:TPU:192 now
where the time goes in v1:
time: 85.5 us; the launch traced here: 85.1 us
  blocking collectives  27.3 us (32%)
  waiting for transfers between devices  21.8 us (25%)
  starting transfers between devices  21.6 us (25%)
  Pallas kernels  9.71 us (11%)
  local copies, waits for them, and re-layouts  4.08 us (5%)
    all_gather x1, blocking collectives, shards(): kv = lax.all_gather(kv, 'yh', axis=0, tiled=True)  27.3 us
    all_to_all x1, waiting for transfers between devices, shards(): parts = lax.all_to_all(parts, ('x', 'yl'), 0, 0, tiled=True)  9.81 us
    ppermute x1, waiting for transfers between devices, shards(): other = lax.ppermute(other, 'zl', [(0, 1), (1, 0)])  7.79 us
    pallas_call x1, Pallas kernels, shards(): pl.pallas_call(functools.partial(attend_kernel, reqs), grid=(NX,), in_spe...  6.65 us
    ppermute x1, starting transfers between devices, shards(): lax.ppermute(stream[0], 'section', [(i, (i + 1) % sections) for i in rang...  6.4 us
    all_to_all x1, starting transfers between devices, shards(): parts = lax.all_to_all(parts, ('x', 'yl'), 0, 0, tiled=True)  5.34 us
    all_to_all x1, starting transfers between devices, shards(): lax.all_to_all(jnp.broadcast_to(query, (group, rows, feats)), ('x', 'yl')...  5.31 us
    ppermute x1, waiting for transfers between devices, shards(): lax.ppermute(stream[0], 'section', [(i, (i + 1) % sections) for i in rang...  4.19 us
  transfers between devices with their start and end apart: 5, of which 3 were waited for; matrix products, arithmetic and copies ran while one was open for 1% of the time, Pallas kernels for 0%

profile of v1, /device:TPU:192, one launch (start us, length us, event | category | flops | bytes accessed | tf_op | source)
XLA Modules:
  0.0 85.1 jit_solution(16398727008748852704)
XLA Ops:
  0.0 1.9 %broadcast_in_dim.11 = bf16[8,128,384]{2,1,0:T(8,128)(2,1)} broadcast(bf16[128,384]{1,0:T(8,128)(2,1)} %bitcast.20), dimensions={1,2} | broadcast | bytes 884736 | tf_op jit(solution)/shard_map/broadcast_in_dim | solution.py:149
  1.9 5.3 %all-to-all-start = ((bf16[8,128,384]{2,1,0:T(8,128)(2,1)}), bf16[8,128,384]{2,1,0:T(8,128)(2,1)S(1)}, u32[]{:S(2)}, u32[]{:S(2)}) async-start(bf16[8,128,384]{2,1,0:T(8,128)(2,1)} %broadcast_in_dim.11), calls=%async_computation | async-start | bytes 1572864 | tf_op jit(solution)/shard_map/all_to_all | solution.py:149
  7.2 0.2 reduce-window.9
  7.4 0.1 pad_add_fusion.1.info_ref
  7.5 0.0 copy-start.3
  7.5 27.3 %all_gather.3.kv_ref = bf16[512,768]{1,0:T(8,128)(2,1)S(1)} all-gather(bf16[128,768]{1,0:T(8,128)(2,1)S(1)} %pad_maximum_fusion.2), channel_id=1, replica_groups=mesh['section'=4,'x'=4,'yh'=4,'yl'=2,'zl'=2,'core'=2] {'yh'}, dimensions={0}, use_global_device_ids=true | all-gather | bytes 983040 | tf_op jit(solution)/shard_map/all_gather | solution.py:151
  34.9 0.0 all-to-all-done.q_ref
  34.9 6.7 %shard_map.100 = bf16[8,400,128]{2,1,0:T(8,128)(2,1)} custom-call(s32[7]{0:T(128)S(1)} %pad_add_fusion.1.info_ref, bf16[8,128,384]{2,1,0:T(8,128)(2,1)S(1)} %all-to-all-done.q_ref, bf16[512,768]{1,0:T(8,128)(2,1)S(1)} %all_gather.3.kv_ref), custom_call_target="tpu_custom_call" | custom-call | tf_op jit(solution)/shard_map/pallas_call | solution.py:154
  41.5 5.3 %all-to-all-start.1 = ((bf16[8,400,128]{2,1,0:T(8,128)(2,1)}), bf16[8,400,128]{2,1,0:T(8,128)(2,1)S(1)}, u32[]{:S(2)}, u32[]{:S(2)}) async-start(bf16[8,400,128]{2,1,0:T(8,128)(2,1)} %shard_map.100), calls=%async_computation.1 | async-start | bytes 1638400 | tf_op jit(solution)/shard_map/all_to_all | solution.py:168
  46.9 0.0 copy-start.7
  46.9 0.4 copy.11
  47.3 0.1 pad_add_fusion.info_ref
  47.4 9.8 %all-to-all-done.1.part_ref = bf16[8,400,128]{2,1,0:T(8,128)(2,1)S(1)} async-done(((bf16[8,400,128]{2,1,0:T(8,128)(2,1)}), bf16[8,400,128]{2,1,0:T(8,128)(2,1)S(1)}, u32[]{:S(2)}, u32[]{:S(2)}) %all-to-all-start.1) | async-done | bytes 819232 | tf_op jit(solution)/shard_map/all_to_all | solution.py:168
  57.2 1.7 %copy-done = bf16[1,384,3072]{2,1,0:T(8,128)(2,1)S(1)} copy-done((bf16[1,384,3072]{2,1,0:T(8,128)(2,1)S(1)}, bf16[1,384,3072]{2,1,0:T(8,128)(2,1)}, u32[]{:S(2)}) %copy-start) | copy-done | bytes 2359320
  58.8 1.4 %shard_map.101 = (bf16[128,1664]{1,0:T(8,128)(2,1)S(1)}, f32[128,1664]{1,0:T(8,128)S(1)}) custom-call(s32[10]{0:T(128)S(1)} %pad_add_fusion.info_ref, bf16[8,400,128]{2,1,0:T(8,128)(2,1)S(1)} %all-to-all-done.1.part_ref, bf16[8,384,64]{2,1,0:T(8,128)(2,1)S(1)} %bitcast.16, bf16[384,3072]{1,0:T(8,128)(2,1)S(1)} %bitcast.17), custom_call_target="tpu_custom_call" | custom-call | tf_op jit(solution)/shard_map/pallas_call | solution.py:171
  60.3 1.9 %collective-permute-start = (bf16[128,1664]{1,0:T(8,128)(2,1)S(1)}, bf16[128,1664]{1,0:T(8,128)(2,1)S(1)}, u32[]{:S(2)}, u32[]{:S(2)}) collective-permute-start(bf16[128,1664]{1,0:T(8,128)(2,1)S(1)} %get-tuple-element.8), channel_id=1, source_target_pairs={{0,1},{1,0},{2,3},{3,2},{4,5},{5,4},{6,7},{7,6},{8,9},{9,8},{10,11... | collective-permute-start | bytes 1277960 | tf_op jit(solution)/shard_map/ppermute | solution.py:179
  62.2 6.4 %collective-permute-start.2 = (bf16[128,768]{1,0:T(8,128)(2,1)S(1)}, bf16[128,768]{1,0:T(8,128)(2,1)S(1)}, u32[]{:S(2)}, u32[]{:S(2)}) collective-permute-start(bf16[128,768]{1,0:T(8,128)(2,1)S(1)} %bitcast.25), channel_id=1, source_target_pairs={{0,128},{128,256},{256,384},{384,0},{1,129},{129,257},{257,385},{3... | collective-permute-start | bytes 589832 | tf_op jit(solution)/shard_map/ppermute | solution.py:147
  68.6 0.0 copy-start.1
  68.7 0.0 copy-start.2
  68.7 0.1 convert_add_fusion
  68.8 2.6 %collective-permute-start.1 = (bf16[128,896]{1,0:T(8,128)(2,1)S(1)}, bf16[128,896]{1,0:T(8,128)(2,1)S(1)}, u32[]{:S(2)}, u32[]{:S(2)}) collective-permute-start(bf16[128,896]{1,0:T(8,128)(2,1)S(1)} %pad_maximum_fusion.1), channel_id=1, source_target_pairs={{0,2},{2,0},{1,3},{3,1},{4,6},{6,4},{5,7},{7,5},{8,10},{10,8},{9,1... | collective-permute-start | bytes 688136 | tf_op jit(solution)/shard_map/ppermute | solution.py:185
  71.5 4.2 %collective-permute-done.2.state_ref = bf16[128,768]{1,0:T(8,128)(2,1)S(1)} collective-permute-done((bf16[128,768]{1,0:T(8,128)(2,1)S(1)}, bf16[128,768]{1,0:T(8,128)(2,1)S(1)}, u32[]{:S(2)}, u32[]{:S(2)}) %collective-permute-start.2) | collective-permute-done | bytes 196640 | tf_op jit(solution)/shard_map/ppermute | solution.py:147
  75.7 7.8 %collective-permute-done.1.other_ref = bf16[128,896]{1,0:T(8,128)(2,1)S(1)} collective-permute-done((bf16[128,896]{1,0:T(8,128)(2,1)S(1)}, bf16[128,896]{1,0:T(8,128)(2,1)S(1)}, u32[]{:S(2)}, u32[]{:S(2)}) %collective-permute-start.1) | collective-permute-done | bytes 229408 | tf_op jit(solution)/shard_map/ppermute | solution.py:185
  83.5 1.6 %shard_map.102 = bf16[128,768]{1,0:T(8,128)(2,1)} custom-call(s32[10]{0:T(128)S(1)} %pad_add_fusion.info_ref, f32[128,896]{1,0:T(8,128)S(1)} %pad_maximum_fusion.mine_ref, bf16[128,896]{1,0:T(8,128)(2,1)S(1)} %collective-permute-done.1.other_ref, bf16[128,768]{1,0:T(8,128)(2,1)S(1)} %collective-permute-done.2.state_ref, f32[4,768]{1,0:T(4,128)S(1)} %bitcast.19, ...), custom_call_target="tpu_custom_call" | custom-call | tf_op jit(solution)/shard_map/pallas_call | solution.py:187
  (21 shorter events, 0.2 us)
Async XLA Ops:
  0.0 7.2 %copy-start.8 = (s32[4]{0:T(128)S(1)}, s32[4]{0:T(128)}, u32[]{:S(2)}) copy-start(s32[4]{0:T(128)} %param.10) | copy-start | bytes 52
  0.0 7.5 %copy-start.5 = (bf16[1,128,384]{2,1,0:T(8,128)(2,1)S(1)}, bf16[1,128,384]{2,1,0:T(8,128)(2,1)}, u32[]{:S(2)}) copy-start(bf16[1,128,384]{2,1,0:T(8,128)(2,1)} %param.13) | copy-start | bytes 294916
  0.0 7.5 %copy-start.4 = (bf16[1,128,384]{2,1,0:T(8,128)(2,1)S(1)}, bf16[1,128,384]{2,1,0:T(8,128)(2,1)}, u32[]{:S(2)}) copy-start(bf16[1,128,384]{2,1,0:T(8,128)(2,1)} %param.14) | copy-start | bytes 294916
  1.9 32.9 %all-to-all-start = ((bf16[8,128,384]{2,1,0:T(8,128)(2,1)}), bf16[8,128,384]{2,1,0:T(8,128)(2,1)S(1)}, u32[]{:S(2)}, u32[]{:S(2)}) async-start(bf16[8,128,384]{2,1,0:T(8,128)(2,1)} %broadcast_in_dim.11), calls=%async_computation | async-start | bytes 1572864 | tf_op jit(solution)/shard_map/all_to_all | solution.py:149
  7.5 39.3 %copy-start.3 = (bf16[1,8,384,64]{2,3,1,0:T(8,128)(2,1)S(1)}, bf16[1,8,384,64]{2,3,1,0:T(8,128)(2,1)}, u32[]{:S(2)}) copy-start(bf16[1,8,384,64]{2,3,1,0:T(8,128)(2,1)} %param.18) | copy-start | bytes 1179652
  34.9 12.4 %copy-start.6 = (s32[4]{0:T(128)S(1)}, s32[4]{0:T(128)}, u32[]{:S(2)}) copy-start(s32[4]{0:T(128)} %param.11) | copy-start | bytes 52
  41.5 15.7 %all-to-all-start.1 = ((bf16[8,400,128]{2,1,0:T(8,128)(2,1)}), bf16[8,400,128]{2,1,0:T(8,128)(2,1)S(1)}, u32[]{:S(2)}, u32[]{:S(2)}) async-start(bf16[8,400,128]{2,1,0:T(8,128)(2,1)} %shard_map.100), calls=%async_computation.1 | async-start | bytes 1638400 | tf_op jit(solution)/shard_map/all_to_all | solution.py:168
  46.9 15.3 %copy-start.7 = (bf16[1,128,768]{2,1,0:T(8,128)(2,1)S(1)}, bf16[1,128,768]{2,1,0:T(8,128)(2,1)}, u32[]{:S(2)}) copy-start(bf16[1,128,768]{2,1,0:T(8,128)(2,1)} %param.15) | copy-start | bytes 589828
  57.2 1.7 %copy-start = (bf16[1,384,3072]{2,1,0:T(8,128)(2,1)S(1)}, bf16[1,384,3072]{2,1,0:T(8,128)(2,1)}, u32[]{:S(2)}) copy-start(bf16[1,384,3072]{2,1,0:T(8,128)(2,1)} %param.17) | copy-start | bytes 7077892
  60.3 8.4 %collective-permute-start = (bf16[128,1664]{1,0:T(8,128)(2,1)S(1)}, bf16[128,1664]{1,0:T(8,128)(2,1)S(1)}, u32[]{:S(2)}, u32[]{:S(2)}) collective-permute-start(bf16[128,1664]{1,0:T(8,128)(2,1)S(1)} %get-tuple-element.8), channel_id=1, source_target_pairs={{0,1},{1,0},{2,3},{3,2},{4,5},{5,4},{6,7},{7,6},{8,9},{9,8},{10,11... | collective-permute-start | bytes 1277960 | tf_op jit(solution)/shard_map/ppermute | solution.py:179
  62.2 13.5 %collective-permute-start.2 = (bf16[128,768]{1,0:T(8,128)(2,1)S(1)}, bf16[128,768]{1,0:T(8,128)(2,1)S(1)}, u32[]{:S(2)}, u32[]{:S(2)}) collective-permute-start(bf16[128,768]{1,0:T(8,128)(2,1)S(1)} %bitcast.25), channel_id=1, source_target_pairs={{0,128},{128,256},{256,384},{384,0},{1,129},{129,257},{257,385},{3... | collective-permute-start | bytes 589832 | tf_op jit(solution)/shard_map/ppermute | solution.py:147
  68.6 14.9 %copy-start.1 = (bf16[1,8,64,768]{3,2,1,0:T(8,128)(2,1)S(1)}, bf16[1,8,64,768]{3,2,1,0:T(8,128)(2,1)}, u32[]{:S(2)}) copy-start(bf16[1,8,64,768]{3,2,1,0:T(8,128)(2,1)} %param.19) | copy-start | bytes 2359300
  68.7 14.9 %copy-start.2 = (f32[1,4,768]{2,1,0:T(4,128)S(1)}, f32[1,4,768]{2,1,0:T(4,128)}, u32[]{:S(2)}) copy-start(f32[1,4,768]{2,1,0:T(4,128)} %param.16) | copy-start | bytes 36868
  68.8 14.7 %collective-permute-start.1 = (bf16[128,896]{1,0:T(8,128)(2,1)S(1)}, bf16[128,896]{1,0:T(8,128)(2,1)S(1)}, u32[]{:S(2)}, u32[]{:S(2)}) collective-permute-start(bf16[128,896]{1,0:T(8,128)(2,1)S(1)} %pad_maximum_fusion.1), channel_id=1, source_target_pairs={{0,2},{2,0},{1,3},{3,1},{4,6},{6,4},{5,7},{7,5},{8,10},{10,8},{9,1... | collective-permute-start | bytes 688136 | tf_op jit(solution)/shard_map/ppermute | solution.py:185

commit v2 on v1

v2 whole, which is shorter than its diff:
```python
import functools
import math

import jax
import jax.numpy as jnp
from jax import lax
from jax.experimental import pallas as pl
from jax.experimental.pallas import tpu as pltpu
from jax.sharding import Mesh, PartitionSpec as P

HEAD = 128
NEG = -1e30
NX, NYH, NYL = 4, 4, 2
NZ, NC = 2, 2
STAT_ROWS = 16
F32 = jnp.float32
BF16 = jnp.bfloat16
VMEM_LIMIT = 48 * 1024 * 1024


def segment_of(position, lengths_ref):
    seg = jnp.zeros(position.shape, jnp.int32)
    end = 0
    for r in range(lengths_ref.shape[0]):
        end = end + lengths_ref[r]
        seg = seg + (position >= end).astype(jnp.int32)
    return seg


def own_segments(rows, lengths_ref):
    first = ((lax.axis_index("x") * NYH + lax.axis_index("yh")) * NYL + lax.axis_index("yl")) * rows
    return segment_of(first + lax.broadcasted_iota(jnp.int32, (rows, 1), 0), lengths_ref)


def spread_kernel(q_ref, out_ref):
    for i in range(out_ref.shape[0]):
        out_ref[i] = q_ref[...]


def attend_kernel(lengths_ref, q_ref, kv_ref, out_ref, kx_ref, vt_ref):
    reqs = lengths_ref.shape[0]
    blocks, rows, feats = out_ref.shape[0], out_ref.shape[2], q_ref.shape[1]
    heads = feats // HEAD
    keys = kv_ref.shape[0]
    my_x, my_yh, my_yl = lax.axis_index("x"), lax.axis_index("yh"), lax.axis_index("yl")
    scale = math.log2(math.e) / math.sqrt(HEAD)

    row = lax.broadcasted_iota(jnp.int32, (keys, HEAD), 0)
    lane = lax.broadcasted_iota(jnp.int32, (keys, HEAD), 1)
    block = row // rows
    place = ((my_x * NYH + block) * NYL + my_yl) * rows + (row - block * rows)
    seg = segment_of(place, lengths_ref)
    bar = jnp.where((lane < reqs) & (lane != seg), NEG, 0.0).astype(BF16)
    for h in range(heads):
        kx_ref[h, :, 0:HEAD] = kv_ref[:, h * HEAD : (h + 1) * HEAD]
        kx_ref[h, :, HEAD : 2 * HEAD] = bar
    vt_ref[...] = kv_ref[:, feats : 2 * feats].T

    n_q = blocks * rows
    span = NYL * rows
    row = lax.broadcasted_iota(jnp.int32, (n_q, HEAD), 0)
    lane = lax.broadcasted_iota(jnp.int32, (n_q, HEAD), 1)
    block = row // span
    place = (block * NYH + my_yh) * span + (row - block * span)
    member = (segment_of(place, lengths_ref) == lane).astype(F32).astype(BF16)
    scores = []
    for h in range(heads):
        queries = jnp.concatenate([q_ref[:, h * HEAD : (h + 1) * HEAD], member], axis=1)
        scores.append(lax.dot_general(kx_ref[h], queries, (((1,), (1,)), ((), ())), preferred_element_type=F32))
    tops = [jnp.max(s, axis=0, keepdims=True) for s in scores]
    weights, totals = [], []
    for h in range(heads):
        weight = jnp.exp2((scores[h] - tops[h]) * scale)
        totals.append(jnp.sum(weight, axis=0, keepdims=True))
        weights.append(weight.astype(BF16))
    high, mid, low = [], [], []
    for h in range(heads):
        part = jnp.dot(vt_ref[h * HEAD : (h + 1) * HEAD, :], weights[h], preferred_element_type=F32)
        part = (part * (1.0 / totals[h])).astype(BF16)
        for i in range(blocks):
            out_ref[i, h * HEAD : (h + 1) * HEAD, :] = part[:, i * rows : (i + 1) * rows]
        level = tops[h] * scale + jnp.log2(totals[h])
        a = level.astype(BF16).astype(F32)
        b = (level - a).astype(BF16).astype(F32)
        high.append(a)
        mid.append(b)
        low.append(level - a - b)
    blank = [jnp.zeros((1, n_q), F32)] * (STAT_ROWS - 3 * heads)
    stats = jnp.concatenate(high + mid + low + blank, axis=0).astype(BF16)
    for i in range(blocks):
        out_ref[i, feats : feats + STAT_ROWS, :] = stats[:, i * rows : (i + 1) * rows]


def project_kernel(lengths_ref, part_ref, down_ref, w_ref, send_ref, keep_ref):
    groups = part_ref.shape[0]
    feats, out_feats = w_ref.shape
    rows = part_ref.shape[2]
    heads = feats // HEAD
    quarter = out_feats // (NZ * NC)
    stat = part_ref[:, feats : feats + STAT_ROWS, :].astype(F32)
    level = stat[:, 0:heads] + stat[:, heads : 2 * heads] + stat[:, 2 * heads : 3 * heads]
    share = jnp.exp2(level - jnp.max(level, axis=0, keepdims=True))
    share = share / jnp.sum(share, axis=0, keepdims=True)
    columns = []
    for h in range(heads):
        acc = jnp.zeros((HEAD, rows), F32)
        for g in range(groups):
            acc = acc + part_ref[g, h * HEAD : (h + 1) * HEAD, :].astype(F32) * share[g, h : h + 1, :]
        columns.append(acc.T.astype(BF16))
    attn = jnp.concatenate(columns, axis=1)

    seg = own_segments(rows, lengths_ref)
    rank = jnp.zeros((rows, down_ref.shape[1]), F32)
    for r in range(lengths_ref.shape[0]):
        mid = lax.dot_general(attn, down_ref[r], (((1,), (1,)), ((), ())), preferred_element_type=F32)
        rank = rank + jnp.where(seg == r, mid, 0.0)
    rank = jnp.concatenate([rank, jnp.zeros((rows, HEAD - rank.shape[1]), F32)], axis=1)
    core = lax.axis_index("core")
    for z in range(NZ):
        for ref, c in ((send_ref, 1 - core), (keep_ref, core)):
            start = pl.multiple_of((z * NC + c) * quarter, quarter)
            product = jnp.dot(attn, w_ref[:, pl.ds(start, quarter)], preferred_element_type=F32)
            ref[:, z * quarter : (z + 1) * quarter] = product.astype(ref.dtype)
    send_ref[:, NZ * quarter : NZ * quarter + HEAD] = rank.astype(send_ref.dtype)
    keep_ref[:, NZ * quarter : NZ * quarter + HEAD] = rank.astype(keep_ref.dtype)


def hold_kernel(adapter_ref, matrix_ref, down_ref, w_ref, chosen_ref):
    w_ref[...] = matrix_ref[...]
    for r in range(chosen_ref.shape[0]):
        chosen_ref[r] = down_ref[adapter_ref[r]]


def fold_kernel(keep_ref, cores_ref, mine_ref, other_ref):
    quarter = mine_ref.shape[1] - HEAD
    core, z = lax.axis_index("core"), lax.axis_index("zl")
    for ref, which in ((other_ref, 1 - z), (mine_ref, z)):
        for cols, at in (
            (pl.ds(pl.multiple_of(which * quarter, quarter), quarter), pl.ds(0, quarter)),
            (pl.ds(NZ * quarter, HEAD), pl.ds(quarter, HEAD)),
        ):
            ref[:, at] = (keep_ref[:, cols] + cores_ref[1 - core, :, cols].astype(F32)).astype(ref.dtype)


def finish_kernel(lengths_ref, adapter_ref, mine_ref, other_ref, state_ref, gate_ref, up_ref, out_ref):
    rows, quarter = out_ref.shape
    ranks = up_ref.shape[1]
    seg = own_segments(rows, lengths_ref)
    there = 1 - lax.axis_index("zl")
    rank = mine_ref[:, quarter : quarter + ranks] + other_ref[there, :, quarter : quarter + ranks].astype(F32)
    rank = rank.astype(BF16).astype(F32)
    branch = mine_ref[:, 0:quarter] + other_ref[there, :, 0:quarter].astype(F32)
    gates = jnp.zeros((rows, quarter), F32)
    for r in range(lengths_ref.shape[0]):
        chosen = jnp.where(seg == r, rank, 0.0).astype(BF16)
        branch = branch + jnp.dot(chosen, up_ref[adapter_ref[r]], preferred_element_type=F32)
        gates = jnp.where(seg == r, gate_ref[r : r + 1, :], gates)
    out_ref[...] = (state_ref[...].astype(F32) + gates * branch).astype(out_ref.dtype)


def shards(lengths, adapter, query, previous_keys, previous_values, stream, gate, output_matrix, adapter_down, adapter_up):
    rows, feats = query.shape[1:]
    quarter = output_matrix.shape[2] // (NZ * NC)
    group = NX * NYL
    smem = pl.BlockSpec(memory_space=pltpu.SMEM)
    vmem = pl.BlockSpec(memory_space=pltpu.VMEM)
    hbm = pl.BlockSpec(memory_space=pl.ANY)
    params = pltpu.CompilerParams(vmem_limit_bytes=VMEM_LIMIT)

    sections = lax.axis_size("section")
    state = lax.ppermute(stream[0], "section", [(i, (i + 1) % sections) for i in range(sections)])

    pair = lax.all_gather(query[0], "yl", axis=0, tiled=True)
    queries = pl.pallas_call(
        spread_kernel,
        in_specs=[vmem],
        out_specs=vmem,
        out_shape=jax.ShapeDtypeStruct((NX, NYL * rows, feats), BF16),
        compiler_params=params,
    )(pair)
    kv = jnp.concatenate([previous_keys[0], previous_values[0]], axis=1)
    queries = lax.all_to_all(queries, "x", 0, 0, tiled=True)
    kv = lax.all_gather(kv, "yh", axis=0, tiled=True)

    keys = NYH * rows
    parts = pl.pallas_call(
        attend_kernel,
        in_specs=[smem, vmem, vmem],
        out_specs=vmem,
        out_shape=jax.ShapeDtypeStruct((group, feats + STAT_ROWS, rows), BF16),
        scratch_shapes=[pltpu.VMEM((feats // HEAD, keys, 2 * HEAD), BF16), pltpu.VMEM((feats, keys), BF16)],
        compiler_params=params,
    )(lengths, queries.reshape(group * rows, feats), kv)
    parts = lax.all_to_all(parts, ("x", "yl"), 0, 0, tiled=True)

    down = jnp.swapaxes(adapter_down[0], 1, 2)
    matrix, down = pl.pallas_call(
        hold_kernel,
        in_specs=[smem, vmem, vmem],
        out_specs=[vmem, vmem],
        out_shape=[
            jax.ShapeDtypeStruct(output_matrix.shape[1:], BF16),
            jax.ShapeDtypeStruct((adapter.shape[0],) + down.shape[1:], BF16),
        ],
        compiler_params=pltpu.CompilerParams(vmem_limit_bytes=32 * 1024 * 1024),
    )(adapter, output_matrix[0], down)
    width = NZ * quarter + HEAD
    send, keep = pl.pallas_call(
        project_kernel,
        in_specs=[smem, vmem, vmem, vmem],
        out_specs=[vmem, vmem],
        out_shape=[jax.ShapeDtypeStruct((rows, width), BF16), jax.ShapeDtypeStruct((rows, width), F32)],
        compiler_params=params,
    )(lengths, parts, down, matrix)
    cores = lax.all_gather(send, "core", axis=0, tiled=False)
    mine, other = pl.pallas_call(
        fold_kernel,
        in_specs=[vmem, vmem],
        out_specs=[vmem, vmem],
        out_shape=[jax.ShapeDtypeStruct((rows, quarter + HEAD), F32), jax.ShapeDtypeStruct((rows, quarter + HEAD), BF16)],
        compiler_params=params,
    )(keep, cores)
    other = lax.all_gather(other, "zl", axis=0, tiled=False)

    out = pl.pallas_call(
        finish_kernel,
        in_specs=[smem, smem] + [vmem] * 5,
        out_specs=vmem,
        out_shape=jax.ShapeDtypeStruct((rows, quarter), BF16),
        compiler_params=params,
    )(lengths, adapter, mine, other, state, gate[0], adapter_up[0])
    return out[None]


def solution(mesh):
    devices = mesh.devices.reshape(mesh.shape["section"], NX, NYH, NYL, NZ, NC)
    fine = Mesh(devices, ("section", "x", "yh", "yl", "zl", "core"))
    seq, head = ("x", "yh", "yl"), ("zl", "core")
    placed = (
        P(),
        P(),
        P("section", seq, head),
        P("section", seq, head),
        P("section", seq, head),
        P("section", seq, head),
        P("section", None, head),
        P("section", head, None),
        P("section", None, head, None),
        P("section", None, None, head),
    )
    return jax.shard_map(shards, mesh=fine, in_specs=placed, out_specs=P("section", seq, head), check_vma=False)
```

time: 85.5 us -> 68.7 us (0.80)
  the two profiles are of different devices: /device:TPU:192 before, /device:TPU:1 now
where the time goes in v2:
time: 68.7 us; the launch traced here: 68.3 us
  blocking collectives  41.9 us (61%)
  starting transfers between devices  13.9 us (20%)
  Pallas kernels  9.43 us (14%)
  local copies, waits for them, and re-layouts  2.69 us (4%)
    all_gather x1, blocking collectives, shards(): kv = lax.all_gather(kv, 'yh', axis=0, tiled=True)  19.4 us
    all_gather x1, blocking collectives, shards(): cores = lax.all_gather(send, 'core', axis=0, tiled=False)  9.79 us
    all_gather x1, blocking collectives, shards(): other = lax.all_gather(other, 'zl', axis=0, tiled=False)  7.49 us
    ppermute x1, starting transfers between devices, shards(): lax.ppermute(stream[0], 'section', [(i, (i + 1) % sections) for i in rang...  5.48 us
    all_gather x1, blocking collectives, shards(): pair = lax.all_gather(query[0], 'yl', axis=0, tiled=True)  5.19 us
    all_to_all x1, starting transfers between devices, shards(): parts = lax.all_to_all(parts, ('x', 'yl'), 0, 0, tiled=True)  4.31 us
    pallas_call x1, Pallas kernels, shards(): pl.pallas_call(attend_kernel, in_specs=[smem, vmem, vmem], out_specs=vmem...  4.18 us
    all_to_all x1, starting transfers between devices, shards(): queries = lax.all_to_all(queries, 'x', 0, 0, tiled=True)  4.14 us
  transfers between devices with their start and end apart: 3, of which 1 were waited for; matrix products, arithmetic and copies ran while one was open for 0% of the time, Pallas kernels for 3%

profile of v2, /device:TPU:1, one launch (start us, length us, event | category | flops | bytes accessed | tf_op | source)
XLA Modules:
  0.0 68.3 jit_solution(16876874602185356061)
XLA Ops:
  0.0 5.2 %all-gather = bf16[1,256,384]{2,1,0:T(8,128)(2,1)S(1)} all-gather(bf16[1,128,384]{2,1,0:T(8,128)(2,1)} %param.12), channel_id=2, replica_groups=mesh['section'=4,'x'=4,'yh'=4,'yl'=2,'zl'=2,'core'=2] {'yl'}, dimensions={1}, use_global_device_ids=true | all-gather | bytes 294912 | tf_op jit(solution)/shard_map/all_gather | solution.py:173
  5.2 1.0 %shard_map.100 = bf16[4,256,384]{2,1,0:T(8,128)(2,1)} custom-call(bf16[256,384]{1,0:T(8,128)(2,1)S(1)} %bitcast.19), custom_call_target="tpu_custom_call" | custom-call | tf_op jit(solution)/shard_map/pallas_call | solution.py:174
  6.2 4.1 %all-to-all-start = ((bf16[4,256,384]{2,1,0:T(8,128)(2,1)}), bf16[4,256,384]{2,1,0:T(8,128)(2,1)S(1)}, u32[]{:S(2)}, u32[]{:S(2)}) async-start(bf16[4,256,384]{2,1,0:T(8,128)(2,1)} %shard_map.100), calls=%async_computation | async-start | bytes 1572864 | tf_op jit(solution)/shard_map/all_to_all | solution.py:182
  10.3 0.0 copy-done.6
  10.3 0.0 copy-start.5
  10.4 19.4 %all_gather.19.kv_ref = bf16[512,768]{1,0:T(8,128)(2,1)S(1)} all-gather(bf16[128,768]{1,0:T(8,128)(2,1)S(1)} %pad_maximum_fusion), channel_id=1, replica_groups=mesh['section'=4,'x'=4,'yh'=4,'yl'=2,'zl'=2,'core'=2] {'yh'}, dimensions={0}, use_global_device_ids=true | all-gather | bytes 983040 | tf_op jit(solution)/shard_map/all_gather | solution.py:183
  29.7 0.0 all-to-all-done
  29.7 4.2 %shard_map.101 = bf16[8,400,128]{2,1,0:T(8,128)(2,1)} custom-call(s32[4]{0:T(128)S(1)} %copy-done.4, bf16[1024,384]{1,0:T(8,128)(2,1)S(1)} %bitcast.15, bf16[512,768]{1,0:T(8,128)(2,1)S(1)} %all_gather.19.kv_ref), custom_call_target="tpu_custom_call" | custom-call | tf_op jit(solution)/shard_map/pallas_call | solution.py:186
  33.9 4.3 %all-to-all-start.1 = ((bf16[8,400,128]{2,1,0:T(8,128)(2,1)}), bf16[8,400,128]{2,1,0:T(8,128)(2,1)S(1)}, u32[]{:S(2)}, u32[]{:S(2)}) async-start(bf16[8,400,128]{2,1,0:T(8,128)(2,1)} %shard_map.101), calls=%async_computation.1 | async-start | bytes 1638400 | tf_op jit(solution)/shard_map/all_to_all | solution.py:194
  38.2 5.5 %collective-permute-start = (bf16[128,768]{1,0:T(8,128)(2,1)}, bf16[128,768]{1,0:T(8,128)(2,1)}, u32[]{:S(2)}, u32[]{:S(2)}) collective-permute-start(bf16[128,768]{1,0:T(8,128)(2,1)} %bitcast.9), channel_id=1, source_target_pairs={{0,128},{128,256},{256,384},{384,0},{1,129},{129,257},{257,385},{3... | collective-permute-start | bytes 589832 | tf_op jit(solution)/shard_map/ppermute | solution.py:171
  43.7 0.0 copy-start
  43.7 1.7 %copy-done = bf16[1,384,3072]{2,1,0:T(8,128)(2,1)S(1)} copy-done((bf16[1,384,3072]{2,1,0:T(8,128)(2,1)S(1)}, bf16[1,384,3072]{2,1,0:T(8,128)(2,1)}, u32[]{:S(2)}) %copy-start) | copy-done | bytes 2359320
  45.4 1.0 %copy-done.2 = bf16[1,8,384,64]{2,3,1,0:T(8,128)(2,1)S(1)} copy-done((bf16[1,8,384,64]{2,3,1,0:T(8,128)(2,1)S(1)}, bf16[1,8,384,64]{2,3,1,0:T(8,128)(2,1)}, u32[]{:S(2)}) %copy-start.2) | copy-done | bytes 393240
  46.4 0.7 %shard_map.102 = (bf16[384,3072]{1,0:T(8,128)(2,1)S(1)}, bf16[4,64,384]{2,1,0:T(8,128)(2,1)S(1)}) custom-call(s32[4]{0:T(128)S(1)} %copy-done.5, bf16[384,3072]{1,0:T(8,128)(2,1)S(1)} %bitcast.16, bf16[8,64,384]{2,1,0:T(8,128)(2,1)S(1)} %bitcast.20), custom_call_target="tpu_custom_call" | custom-call | tf_op jit(solution)/shard_map/pallas_call | solution.py:197
  47.1 0.3 all-to-all-done.1.part_ref
  47.4 1.4 %shard_map.103 = (bf16[128,1664]{1,0:T(8,128)(2,1)S(1)}, f32[128,1664]{1,0:T(8,128)S(1)}) custom-call(s32[4]{0:T(128)S(1)} %copy-done.4, bf16[8,400,128]{2,1,0:T(8,128)(2,1)S(1)} %all-to-all-done.1.part_ref, bf16[4,64,384]{2,1,0:T(8,128)(2,1)S(1)} %get-tuple-element.11.down_ref, bf16[384,3072]{1,0:T(8,128)(2,1)S(1)} %get-tuple-element.12.w_ref), custom_call_target="tpu_custom_call" | custom-call | tf_op jit(solution)/shard_map/pallas_call | solution.py:208
  48.8 0.0 copy-start.1
  48.8 0.0 copy-start.3
  48.9 9.8 %all-gather.1 = bf16[256,1664]{1,0:T(8,128)(2,1)S(1)} all-gather(bf16[128,1664]{1,0:T(8,128)(2,1)S(1)} %get-tuple-element.14), channel_id=3, replica_groups=mesh['section'=4,'x'=4,'yh'=4,'yl'=2,'zl'=2,'core'=2] {'core'}, dimensions={0}, use_global_device_ids=true | all-gather | bytes 1277952 | tf_op jit(solution)/shard_map/all_gather | solution.py:215
  58.6 0.1 shard_map.104
  58.7 7.5 %all-gather.2 = bf16[256,896]{1,0:T(8,128)(2,1)S(1)} all-gather(bf16[128,896]{1,0:T(8,128)(2,1)S(1)} %get-tuple-element.16), channel_id=4, replica_groups=mesh['section'=4,'x'=4,'yh'=4,'yl'=2,'zl'=2,'core'=2] {'zl'}, dimensions={0}, use_global_device_ids=true | all-gather | bytes 688128 | tf_op jit(solution)/shard_map/all_gather | solution.py:223
  66.2 0.0 collective-permute-done.state_ref
  66.2 0.0 copy-done.1
  66.2 2.0 %shard_map.105 = bf16[128,768]{1,0:T(8,128)(2,1)} custom-call(s32[4]{0:T(128)S(1)} %copy-done.4, s32[4]{0:T(128)S(1)} %copy-done.5, f32[128,896]{1,0:T(8,128)S(1)} %get-tuple-element.15.mine_ref, bf16[2,128,896]{2,1,0:T(8,128)(2,1)S(1)} %bitcast.17, bf16[128,768]{1,0:T(8,128)(2,1)} %collective-permute-done.state_ref, f32[4,768]{1,0:T(4,128)S(1)} %bitcast.21, ...), custom_call_target="tpu_custom_call" | custom-call | tf_op jit(solution)/shard_map/pallas_call | solution.py:225
  (9 shorter events, 0.0 us)
Async XLA Ops:
  0.0 10.3 %copy-start.6 = (bf16[1,128,384]{2,1,0:T(8,128)(2,1)S(1)}, bf16[1,128,384]{2,1,0:T(8,128)(2,1)}, u32[]{:S(2)}) copy-start(bf16[1,128,384]{2,1,0:T(8,128)(2,1)} %param.14) | copy-start | bytes 294916
  0.0 10.3 %copy-start.7 = (bf16[1,128,384]{2,1,0:T(8,128)(2,1)S(1)}, bf16[1,128,384]{2,1,0:T(8,128)(2,1)}, u32[]{:S(2)}) copy-start(bf16[1,128,384]{2,1,0:T(8,128)(2,1)} %param.13) | copy-start | bytes 294916
  0.0 29.7 %copy-start.4 = (s32[4]{0:T(128)S(1)}, s32[4]{0:T(128)}, u32[]{:S(2)}) copy-start(s32[4]{0:T(128)} %lengths_ref.5) | copy-start | bytes 52
  6.2 23.5 %all-to-all-start = ((bf16[4,256,384]{2,1,0:T(8,128)(2,1)}), bf16[4,256,384]{2,1,0:T(8,128)(2,1)S(1)}, u32[]{:S(2)}, u32[]{:S(2)}) async-start(bf16[4,256,384]{2,1,0:T(8,128)(2,1)} %shard_map.100), calls=%async_computation | async-start | bytes 1572864 | tf_op jit(solution)/shard_map/all_to_all | solution.py:182
  10.3 33.4 %copy-start.5 = (s32[4]{0:T(128)S(1)}, s32[4]{0:T(128)}, u32[]{:S(2)}) copy-start(s32[4]{0:T(128)} %adapter_ref.3) | copy-start | bytes 52
  33.9 13.5 %all-to-all-start.1 = ((bf16[8,400,128]{2,1,0:T(8,128)(2,1)}), bf16[8,400,128]{2,1,0:T(8,128)(2,1)S(1)}, u32[]{:S(2)}, u32[]{:S(2)}) async-start(bf16[8,400,128]{2,1,0:T(8,128)(2,1)} %shard_map.101), calls=%async_computation.1 | async-start | bytes 1638400 | tf_op jit(solution)/shard_map/all_to_all | solution.py:194
  38.2 28.0 %collective-permute-start = (bf16[128,768]{1,0:T(8,128)(2,1)}, bf16[128,768]{1,0:T(8,128)(2,1)}, u32[]{:S(2)}, u32[]{:S(2)}) collective-permute-start(bf16[128,768]{1,0:T(8,128)(2,1)} %bitcast.9), channel_id=1, source_target_pairs={{0,128},{128,256},{256,384},{384,0},{1,129},{129,257},{257,385},{3... | collective-permute-start | bytes 589832 | tf_op jit(solution)/shard_map/ppermute | solution.py:171
  43.7 1.7 %copy-start = (bf16[1,384,3072]{2,1,0:T(8,128)(2,1)S(1)}, bf16[1,384,3072]{2,1,0:T(8,128)(2,1)}, u32[]{:S(2)}) copy-start(bf16[1,384,3072]{2,1,0:T(8,128)(2,1)} %param.17) | copy-start | bytes 7077892
  45.4 1.0 %copy-start.2 = (bf16[1,8,384,64]{2,3,1,0:T(8,128)(2,1)S(1)}, bf16[1,8,384,64]{2,3,1,0:T(8,128)(2,1)}, u32[]{:S(2)}) copy-start(bf16[1,8,384,64]{2,3,1,0:T(8,128)(2,1)} %param.18) | copy-start | bytes 1179652
  48.8 17.4 %copy-start.1 = (bf16[1,8,64,768]{3,2,1,0:T(8,128)(2,1)S(1)}, bf16[1,8,64,768]{3,2,1,0:T(8,128)(2,1)}, u32[]{:S(2)}) copy-start(bf16[1,8,64,768]{3,2,1,0:T(8,128)(2,1)} %param.19) | copy-start | bytes 2359300
  48.8 17.4 %copy-start.3 = (f32[1,4,768]{2,1,0:T(4,128)S(1)}, f32[1,4,768]{2,1,0:T(4,128)}, u32[]{:S(2)}) copy-start(f32[1,4,768]{2,1,0:T(4,128)} %param.16) | copy-start | bytes 36868

commit v3 on v2

--- a/solution.py
+++ b/solution.py
@@ -15,7 +15,7 @@
 STAT_ROWS = 16
 F32 = jnp.float32
 BF16 = jnp.bfloat16
-VMEM_LIMIT = 48 * 1024 * 1024
+VMEM_LIMIT = 32 * 1024 * 1024
 
 
 def segment_of(position, lengths_ref):
@@ -27,59 +27,75 @@
     return seg
 
 
+def spans(lengths_ref):
+    lane = lax.broadcasted_iota(jnp.int32, (1, HEAD), 1)
+    start = jnp.zeros((1, HEAD), jnp.int32)
+    stop = jnp.full((1, HEAD), jnp.iinfo(jnp.int32).max, jnp.int32)
+    end = 0
+    for r in range(lengths_ref.shape[0]):
+        start = jnp.where(lane == r, end, start)
+        end = end + lengths_ref[r]
+        stop = jnp.where(lane == r, end, stop)
+    return start, stop
+
+
 def own_segments(rows, lengths_ref):
     first = ((lax.axis_index("x") * NYH + lax.axis_index("yh")) * NYL + lax.axis_index("yl")) * rows
     return segment_of(first + lax.broadcasted_iota(jnp.int32, (rows, 1), 0), lengths_ref)
 
 
-def spread_kernel(q_ref, out_ref):
-    for i in range(out_ref.shape[0]):
-        out_ref[i] = q_ref[...]
-
-
-def attend_kernel(lengths_ref, q_ref, kv_ref, out_ref, kx_ref, vt_ref):
-    reqs = lengths_ref.shape[0]
+def spread_kernel(q_ref, out_ref, sems):
+    copies = [pltpu.make_async_copy(q_ref, out_ref.at[i], sems.at[i]) for i in range(out_ref.shape[0])]
+    for copy in copies:
+        copy.start()
+    for copy in copies:
+        copy.wait()
+
+
+def attend_kernel(lengths_ref, q_ref, kv_ref, result_ref, vt_ref, out_ref, sems):
     blocks, rows, feats = out_ref.shape[0], out_ref.shape[2], q_ref.shape[1]
     heads = feats // HEAD
     keys = kv_ref.shape[0]
     my_x, my_yh, my_yl = lax.axis_index("x"), lax.axis_index("yh"), lax.axis_index("yl")
     scale = math.log2(math.e) / math.sqrt(HEAD)
 
+    start, stop = spans(lengths_ref)
     row = lax.broadcasted_iota(jnp.int32, (keys, HEAD), 0)
-    lane = lax.broadcasted_iota(jnp.int32, (keys, HEAD), 1)
     block = row // rows
     place = ((my_x * NYH + block) * NYL + my_yl) * rows + (row - block * rows)
-    seg = segment_of(place, lengths_ref)
-    bar = jnp.where((lane < reqs) & (lane != seg), NEG, 0.0).astype(BF16)
-    for h in range(heads):
-        kx_ref[h, :, 0:HEAD] = kv_ref[:, h * HEAD : (h + 1) * HEAD]
-        kx_ref[h, :, HEAD : 2 * HEAD] = bar
+    bar = jnp.where((place >= start) & (place < stop), 0.0, NEG).astype(BF16)
     vt_ref[...] = kv_ref[:, feats : 2 * feats].T
 
     n_q = blocks * rows
     span = NYL * rows
     row = lax.broadcasted_iota(jnp.int32, (n_q, HEAD), 0)
-    lane = lax.broadcasted_iota(jnp.int32, (n_q, HEAD), 1)
     block = row // span
     place = (block * NYH + my_yh) * span + (row - block * span)
-    member = (segment_of(place, lengths_ref) == lane).astype(F32).astype(BF16)
+    member = jnp.where((place >= start) & (place < stop), 1.0, 0.0).astype(BF16)
     scores = []
     for h in range(heads):
-        queries = jnp.concatenate([q_ref[:, h * HEAD : (h + 1) * HEAD], member], axis=1)
-        scores.append(lax.dot_general(kx_ref[h], queries, (((1,), (1,)), ((), ())), preferred_element_type=F32))
-    tops = [jnp.max(s, axis=0, keepdims=True) for s in scores]
-    weights, totals = [], []
-    for h in range(heads):
-        weight = jnp.exp2((scores[h] - tops[h]) * scale)
-        totals.append(jnp.sum(weight, axis=0, keepdims=True))
-        weights.append(weight.astype(BF16))
+        at = slice(h * HEAD, (h + 1) * HEAD)
+        these = jnp.concatenate([kv_ref[:, at], bar], axis=1)
+        queries = jnp.concatenate([q_ref[:, at], member], axis=1)
+        scores.append(lax.dot_general(these, queries, (((1,), (1,)), ((), ())), preferred_element_type=F32))
+    copies = []
+
+    def send(start, size):
+        at = (slice(None), pl.ds(start, size))
+        copies.append(pltpu.make_async_copy(out_ref.at[at], result_ref.at[at], sems.at[len(copies)]))
+        copies[-1].start()
+
     high, mid, low = [], [], []
     for h in range(heads):
-        part = jnp.dot(vt_ref[h * HEAD : (h + 1) * HEAD, :], weights[h], preferred_element_type=F32)
-        part = (part * (1.0 / totals[h])).astype(BF16)
+        top = jnp.max(scores[h], axis=0, keepdims=True)
+        weight = jnp.exp2((scores[h] - top) * scale)
+        total = jnp.sum(weight, axis=0, keepdims=True)
+        part = jnp.dot(vt_ref[h * HEAD : (h + 1) * HEAD, :], weight.astype(BF16), preferred_element_type=F32)
+        part = (part * (1.0 / total)).astype(BF16)
         for i in range(blocks):
             out_ref[i, h * HEAD : (h + 1) * HEAD, :] = part[:, i * rows : (i + 1) * rows]
-        level = tops[h] * scale + jnp.log2(totals[h])
+        send(h * HEAD, HEAD)
+        level = top * scale + jnp.log2(total)
         a = level.astype(BF16).astype(F32)
         b = (level - a).astype(BF16).astype(F32)
         high.append(a)
@@ -89,6 +105,9 @@
     stats = jnp.concatenate(high + mid + low + blank, axis=0).astype(BF16)
     for i in range(blocks):
         out_ref[i, feats : feats + STAT_ROWS, :] = stats[:, i * rows : (i + 1) * rows]
+    send(feats, STAT_ROWS)
+    for copy in copies:
+        copy.wait()
 
 
 def project_kernel(lengths_ref, part_ref, down_ref, w_ref, send_ref, keep_ref):
@@ -114,7 +133,7 @@
     for r in range(lengths_ref.shape[0]):
         mid = lax.dot_general(attn, down_ref[r], (((1,), (1,)), ((), ())), preferred_element_type=F32)
         rank = rank + jnp.where(seg == r, mid, 0.0)
-    rank = jnp.concatenate([rank, jnp.zeros((rows, HEAD - rank.shape[1]), F32)], axis=1)
+    rank = jnp.concatenate([rank] * (HEAD // rank.shape[1]), axis=1)
     core = lax.axis_index("core")
     for z in range(NZ):
         for ref, c in ((send_ref, 1 - core), (keep_ref, core)):
@@ -144,17 +163,20 @@
 
 def finish_kernel(lengths_ref, adapter_ref, mine_ref, other_ref, state_ref, gate_ref, up_ref, out_ref):
     rows, quarter = out_ref.shape
+    reqs = lengths_ref.shape[0]
     ranks = up_ref.shape[1]
     seg = own_segments(rows, lengths_ref)
     there = 1 - lax.axis_index("zl")
-    rank = mine_ref[:, quarter : quarter + ranks] + other_ref[there, :, quarter : quarter + ranks].astype(F32)
-    rank = rank.astype(BF16).astype(F32)
+    rank = mine_ref[:, quarter : quarter + HEAD] + other_ref[there, :, quarter : quarter + HEAD].astype(F32)
+    rank = jnp.concatenate([rank] * (reqs * ranks // HEAD), axis=1)
+    owner = lax.broadcasted_iota(jnp.int32, rank.shape, 1) // ranks
+    rank = jnp.where(seg == owner, rank, 0.0).astype(BF16)
+    ups = jnp.concatenate([up_ref[adapter_ref[r]] for r in range(reqs)], axis=0)
+    gates = jnp.zeros((rows, quarter), F32)
+    for r in range(reqs):
+        gates = jnp.where(seg == r, gate_ref[r : r + 1, :], gates)
     branch = mine_ref[:, 0:quarter] + other_ref[there, :, 0:quarter].astype(F32)
-    gates = jnp.zeros((rows, quarter), F32)
-    for r in range(lengths_ref.shape[0]):
-        chosen = jnp.where(seg == r, rank, 0.0).astype(BF16)
-        branch = branch + jnp.dot(chosen, up_ref[adapter_ref[r]], preferred_element_type=F32)
-        gates = jnp.where(seg == r, gate_ref[r : r + 1, :], gates)
+    branch = branch + jnp.dot(rank, ups, preferred_element_type=F32)
     out_ref[...] = (state_ref[...].astype(F32) + gates * branch).astype(out_ref.dtype)
 
 
@@ -174,8 +196,9 @@
     queries = pl.pallas_call(
         spread_kernel,
         in_specs=[vmem],
-        out_specs=vmem,
+        out_specs=hbm,
         out_shape=jax.ShapeDtypeStruct((NX, NYL * rows, feats), BF16),
+        scratch_shapes=[pltpu.SemaphoreType.DMA((NX,))],
         compiler_params=params,
     )(pair)
     kv = jnp.concatenate([previous_keys[0], previous_values[0]], axis=1)
@@ -186,9 +209,13 @@
     parts = pl.pallas_call(
         attend_kernel,
         in_specs=[smem, vmem, vmem],
-        out_specs=vmem,
+        out_specs=hbm,
         out_shape=jax.ShapeDtypeStruct((group, feats + STAT_ROWS, rows), BF16),
-        scratch_shapes=[pltpu.VMEM((feats // HEAD, keys, 2 * HEAD), BF16), pltpu.VMEM((feats, keys), BF16)],
+        scratch_shapes=[
+            pltpu.VMEM((feats, keys), BF16),
+            pltpu.VMEM((group, feats + STAT_ROWS, rows), BF16),
+            pltpu.SemaphoreType.DMA((feats // HEAD + 1,)),
+        ],
         compiler_params=params,
     )(lengths, queries.reshape(group * rows, feats), kv)
     parts = lax.all_to_all(parts, ("x", "yl"), 0, 0, tiled=True)
@@ -202,7 +229,7 @@
             jax.ShapeDtypeStruct(output_matrix.shape[1:], BF16),
             jax.ShapeDtypeStruct((adapter.shape[0],) + down.shape[1:], BF16),
         ],
-        compiler_params=pltpu.CompilerParams(vmem_limit_bytes=32 * 1024 * 1024),
+        compiler_params=pltpu.CompilerParams(vmem_limit_bytes=VMEM_LIMIT),
     )(adapter, output_matrix[0], down)
     width = NZ * quarter + HEAD
     send, keep = pl.pallas_call(

time: 68.7 us -> 68.1 us (level)
  no operation moved by 1% of the time
where the time goes in v3:
time: 68.1 us; the launch traced here: 67.7 us
  blocking collectives  41.9 us (62%)
  starting transfers between devices  13.9 us (20%)
  Pallas kernels  8.79 us (13%)
  local copies, waits for them, and re-layouts  2.69 us (4%)
    all_gather x1, blocking collectives, shards(): kv = lax.all_gather(kv, 'yh', axis=0, tiled=True)  19.4 us
    all_gather x1, blocking collectives, shards(): cores = lax.all_gather(send, 'core', axis=0, tiled=False)  9.8 us
    all_gather x1, blocking collectives, shards(): other = lax.all_gather(other, 'zl', axis=0, tiled=False)  7.49 us
    ppermute x1, starting transfers between devices, shards(): lax.ppermute(stream[0], 'section', [(i, (i + 1) % sections) for i in rang...  5.48 us
    all_gather x1, blocking collectives, shards(): pair = lax.all_gather(query[0], 'yl', axis=0, tiled=True)  5.19 us
    all_to_all x1, starting transfers between devices, shards(): parts = lax.all_to_all(parts, ('x', 'yl'), 0, 0, tiled=True)  4.31 us
    all_to_all x1, starting transfers between devices, shards(): queries = lax.all_to_all(queries, 'x', 0, 0, tiled=True)  4.15 us
    pallas_call x1, Pallas kernels, shards(): pl.pallas_call(attend_kernel, in_specs=[smem, vmem, vmem], out_specs=hbm,...  3.73 us
  transfers between devices with their start and end apart: 3, of which 1 were waited for; matrix products, arithmetic and copies ran while one was open for 0% of the time, Pallas kernels for 3%

profile of v3, /device:TPU:1, one launch (start us, length us, event | category | flops | bytes accessed | tf_op | source)
XLA Modules:
  0.0 67.7 jit_solution(1023292695652142359)
XLA Ops:
  0.0 5.2 %all-gather = bf16[1,256,384]{2,1,0:T(8,128)(2,1)S(1)} all-gather(bf16[1,128,384]{2,1,0:T(8,128)(2,1)} %param.12), channel_id=2, replica_groups=mesh['section'=4,'x'=4,'yh'=4,'yl'=2,'zl'=2,'core'=2] {'yl'}, dimensions={1}, use_global_device_ids=true | all-gather | bytes 294912 | tf_op jit(solution)/shard_map/all_gather | solution.py:195
  5.2 0.9 %shard_map.100 = bf16[4,256,384]{2,1,0:T(8,128)(2,1)} custom-call(bf16[256,384]{1,0:T(8,128)(2,1)S(1)} %bitcast.19), custom_call_target="tpu_custom_call" | custom-call | tf_op jit(solution)/shard_map/pallas_call | solution.py:196
  6.2 4.1 %all-to-all-start = ((bf16[4,256,384]{2,1,0:T(8,128)(2,1)}), bf16[4,256,384]{2,1,0:T(8,128)(2,1)S(1)}, u32[]{:S(2)}, u32[]{:S(2)}) async-start(bf16[4,256,384]{2,1,0:T(8,128)(2,1)} %shard_map.100), calls=%async_computation | async-start | bytes 1572864 | tf_op jit(solution)/shard_map/all_to_all | solution.py:205
  10.3 0.0 copy-start.5
  10.3 19.4 %all_gather.19.kv_ref = bf16[512,768]{1,0:T(8,128)(2,1)S(1)} all-gather(bf16[128,768]{1,0:T(8,128)(2,1)S(1)} %pad_maximum_fusion), channel_id=1, replica_groups=mesh['section'=4,'x'=4,'yh'=4,'yl'=2,'zl'=2,'core'=2] {'yh'}, dimensions={0}, use_global_device_ids=true | all-gather | bytes 983040 | tf_op jit(solution)/shard_map/all_gather | solution.py:206
  29.7 0.0 all-to-all-done
  29.7 0.0 copy-done.4
  29.7 3.7 %shard_map.101 = bf16[8,400,128]{2,1,0:T(8,128)(2,1)} custom-call(s32[4]{0:T(128)S(1)} %copy-done.4, bf16[1024,384]{1,0:T(8,128)(2,1)S(1)} %bitcast.15, bf16[512,768]{1,0:T(8,128)(2,1)S(1)} %all_gather.19.kv_ref), custom_call_target="tpu_custom_call" | custom-call | tf_op jit(solution)/shard_map/pallas_call | solution.py:209
  33.5 4.3 %all-to-all-start.1 = ((bf16[8,400,128]{2,1,0:T(8,128)(2,1)}), bf16[8,400,128]{2,1,0:T(8,128)(2,1)S(1)}, u32[]{:S(2)}, u32[]{:S(2)}) async-start(bf16[8,400,128]{2,1,0:T(8,128)(2,1)} %shard_map.101), calls=%async_computation.1 | async-start | bytes 1638400 | tf_op jit(solution)/shard_map/all_to_all | solution.py:221
  37.8 5.5 %collective-permute-start = (bf16[128,768]{1,0:T(8,128)(2,1)}, bf16[128,768]{1,0:T(8,128)(2,1)}, u32[]{:S(2)}, u32[]{:S(2)}) collective-permute-start(bf16[128,768]{1,0:T(8,128)(2,1)} %bitcast.9), channel_id=1, source_target_pairs={{0,128},{128,256},{256,384},{384,0},{1,129},{129,257},{257,385},{3... | collective-permute-start | bytes 589832 | tf_op jit(solution)/shard_map/ppermute | solution.py:193
  43.3 0.0 copy-start
  43.3 1.7 %copy-done = bf16[1,384,3072]{2,1,0:T(8,128)(2,1)S(1)} copy-done((bf16[1,384,3072]{2,1,0:T(8,128)(2,1)S(1)}, bf16[1,384,3072]{2,1,0:T(8,128)(2,1)}, u32[]{:S(2)}) %copy-start) | copy-done | bytes 2359320
  44.9 1.0 %copy-done.2 = bf16[1,8,384,64]{2,3,1,0:T(8,128)(2,1)S(1)} copy-done((bf16[1,8,384,64]{2,3,1,0:T(8,128)(2,1)S(1)}, bf16[1,8,384,64]{2,3,1,0:T(8,128)(2,1)}, u32[]{:S(2)}) %copy-start.2) | copy-done | bytes 393240
  45.9 0.7 %shard_map.102 = (bf16[384,3072]{1,0:T(8,128)(2,1)S(1)}, bf16[4,64,384]{2,1,0:T(8,128)(2,1)S(1)}) custom-call(s32[4]{0:T(128)S(1)} %copy-done.5, bf16[384,3072]{1,0:T(8,128)(2,1)S(1)} %bitcast.16, bf16[8,64,384]{2,1,0:T(8,128)(2,1)S(1)} %bitcast.20), custom_call_target="tpu_custom_call" | custom-call | tf_op jit(solution)/shard_map/pallas_call | solution.py:224
  46.6 0.3 all-to-all-done.1.part_ref
  46.9 1.4 %shard_map.103 = (bf16[128,1664]{1,0:T(8,128)(2,1)S(1)}, f32[128,1664]{1,0:T(8,128)S(1)}) custom-call(s32[4]{0:T(128)S(1)} %copy-done.4, bf16[8,400,128]{2,1,0:T(8,128)(2,1)S(1)} %all-to-all-done.1.part_ref, bf16[4,64,384]{2,1,0:T(8,128)(2,1)S(1)} %get-tuple-element.11.down_ref, bf16[384,3072]{1,0:T(8,128)(2,1)S(1)} %get-tuple-element.12.w_ref), custom_call_target="tpu_custom_call" | custom-call | tf_op jit(solution)/shard_map/pallas_call | solution.py:235
  48.4 0.0 copy-start.1
  48.4 0.0 copy-start.3
  48.4 9.8 %all-gather.1 = bf16[256,1664]{1,0:T(8,128)(2,1)S(1)} all-gather(bf16[128,1664]{1,0:T(8,128)(2,1)S(1)} %get-tuple-element.14), channel_id=3, replica_groups=mesh['section'=4,'x'=4,'yh'=4,'yl'=2,'zl'=2,'core'=2] {'core'}, dimensions={0}, use_global_device_ids=true | all-gather | bytes 1277952 | tf_op jit(solution)/shard_map/all_gather | solution.py:242
  58.2 0.1 shard_map.104
  58.3 7.5 %all-gather.2 = bf16[256,896]{1,0:T(8,128)(2,1)S(1)} all-gather(bf16[128,896]{1,0:T(8,128)(2,1)S(1)} %get-tuple-element.16), channel_id=4, replica_groups=mesh['section'=4,'x'=4,'yh'=4,'yl'=2,'zl'=2,'core'=2] {'zl'}, dimensions={0}, use_global_device_ids=true | all-gather | bytes 688128 | tf_op jit(solution)/shard_map/all_gather | solution.py:250
  65.8 0.0 collective-permute-done.state_ref
  65.8 0.0 copy-done.1
  65.8 1.9 %shard_map.105 = bf16[128,768]{1,0:T(8,128)(2,1)} custom-call(s32[4]{0:T(128)S(1)} %copy-done.4, s32[4]{0:T(128)S(1)} %copy-done.5, f32[128,896]{1,0:T(8,128)S(1)} %get-tuple-element.15.mine_ref, bf16[2,128,896]{2,1,0:T(8,128)(2,1)S(1)} %bitcast.17, bf16[128,768]{1,0:T(8,128)(2,1)} %collective-permute-done.state_ref, f32[4,768]{1,0:T(4,128)S(1)} %bitcast.21, ...), custom_call_target="tpu_custom_call" | custom-call | tf_op jit(solution)/shard_map/pallas_call | solution.py:252
  (9 shorter events, 0.0 us)
Async XLA Ops:
  0.0 10.3 %copy-start.6 = (bf16[1,128,384]{2,1,0:T(8,128)(2,1)S(1)}, bf16[1,128,384]{2,1,0:T(8,128)(2,1)}, u32[]{:S(2)}) copy-start(bf16[1,128,384]{2,1,0:T(8,128)(2,1)} %param.14) | copy-start | bytes 294916
  0.0 10.3 %copy-start.7 = (bf16[1,128,384]{2,1,0:T(8,128)(2,1)S(1)}, bf16[1,128,384]{2,1,0:T(8,128)(2,1)}, u32[]{:S(2)}) copy-start(bf16[1,128,384]{2,1,0:T(8,128)(2,1)} %param.13) | copy-start | bytes 294916
  0.0 29.7 %copy-start.4 = (s32[4]{0:T(128)S(1)}, s32[4]{0:T(128)}, u32[]{:S(2)}) copy-start(s32[4]{0:T(128)} %lengths_ref.5) | copy-start | bytes 52
  6.2 23.6 %all-to-all-start = ((bf16[4,256,384]{2,1,0:T(8,128)(2,1)}), bf16[4,256,384]{2,1,0:T(8,128)(2,1)S(1)}, u32[]{:S(2)}, u32[]{:S(2)}) async-start(bf16[4,256,384]{2,1,0:T(8,128)(2,1)} %shard_map.100), calls=%async_computation | async-start | bytes 1572864 | tf_op jit(solution)/shard_map/all_to_all | solution.py:205
  10.3 32.9 %copy-start.5 = (s32[4]{0:T(128)S(1)}, s32[4]{0:T(128)}, u32[]{:S(2)}) copy-start(s32[4]{0:T(128)} %adapter_ref.3) | copy-start | bytes 52
  33.5 13.5 %all-to-all-start.1 = ((bf16[8,400,128]{2,1,0:T(8,128)(2,1)}), bf16[8,400,128]{2,1,0:T(8,128)(2,1)S(1)}, u32[]{:S(2)}, u32[]{:S(2)}) async-start(bf16[8,400,128]{2,1,0:T(8,128)(2,1)} %shard_map.101), calls=%async_computation.1 | async-start | bytes 1638400 | tf_op jit(solution)/shard_map/all_to_all | solution.py:221
  37.8 28.0 %collective-permute-start = (bf16[128,768]{1,0:T(8,128)(2,1)}, bf16[128,768]{1,0:T(8,128)(2,1)}, u32[]{:S(2)}, u32[]{:S(2)}) collective-permute-start(bf16[128,768]{1,0:T(8,128)(2,1)} %bitcast.9), channel_id=1, source_target_pairs={{0,128},{128,256},{256,384},{384,0},{1,129},{129,257},{257,385},{3... | collective-permute-start | bytes 589832 | tf_op jit(solution)/shard_map/ppermute | solution.py:193
  43.3 1.7 %copy-start = (bf16[1,384,3072]{2,1,0:T(8,128)(2,1)S(1)}, bf16[1,384,3072]{2,1,0:T(8,128)(2,1)}, u32[]{:S(2)}) copy-start(bf16[1,384,3072]{2,1,0:T(8,128)(2,1)} %param.17) | copy-start | bytes 7077892
  44.9 1.0 %copy-start.2 = (bf16[1,8,384,64]{2,3,1,0:T(8,128)(2,1)S(1)}, bf16[1,8,384,64]{2,3,1,0:T(8,128)(2,1)}, u32[]{:S(2)}) copy-start(bf16[1,8,384,64]{2,3,1,0:T(8,128)(2,1)} %param.18) | copy-start | bytes 1179652
  48.4 17.4 %copy-start.1 = (bf16[1,8,64,768]{3,2,1,0:T(8,128)(2,1)S(1)}, bf16[1,8,64,768]{3,2,1,0:T(8,128)(2,1)}, u32[]{:S(2)}) copy-start(bf16[1,8,64,768]{3,2,1,0:T(8,128)(2,1)} %param.19) | copy-start | bytes 2359300
  48.4 17.4 %copy-start.3 = (f32[1,4,768]{2,1,0:T(4,128)S(1)}, f32[1,4,768]{2,1,0:T(4,128)}, u32[]{:S(2)}) copy-start(f32[1,4,768]{2,1,0:T(4,128)} %param.16) | copy-start | bytes 36868

commit v4 on v3

--- a/solution.py
+++ b/solution.py
@@ -93,7 +93,7 @@
         part = jnp.dot(vt_ref[h * HEAD : (h + 1) * HEAD, :], weight.astype(BF16), preferred_element_type=F32)
         part = (part * (1.0 / total)).astype(BF16)
         for i in range(blocks):
-            out_ref[i, h * HEAD : (h + 1) * HEAD, :] = part[:, i * rows : (i + 1) * rows]
+            out_ref[(i % NYL) * NX + i // NYL, h * HEAD : (h + 1) * HEAD, :] = part[:, i * rows : (i + 1) * rows]
         send(h * HEAD, HEAD)
         level = top * scale + jnp.log2(total)
         a = level.astype(BF16).astype(F32)
@@ -104,7 +104,7 @@
     blank = [jnp.zeros((1, n_q), F32)] * (STAT_ROWS - 3 * heads)
     stats = jnp.concatenate(high + mid + low + blank, axis=0).astype(BF16)
     for i in range(blocks):
-        out_ref[i, feats : feats + STAT_ROWS, :] = stats[:, i * rows : (i + 1) * rows]
+        out_ref[(i % NYL) * NX + i // NYL, feats : feats + STAT_ROWS, :] = stats[:, i * rows : (i + 1) * rows]
     send(feats, STAT_ROWS)
     for copy in copies:
         copy.wait()
@@ -218,7 +218,7 @@
         ],
         compiler_params=params,
     )(lengths, queries.reshape(group * rows, feats), kv)
-    parts = lax.all_to_all(parts, ("x", "yl"), 0, 0, tiled=True)
+    parts = lax.all_to_all(parts, ("yl", "x"), 0, 0, tiled=True)
 
     down = jnp.swapaxes(adapter_down[0], 1, 2)
     matrix, down = pl.pallas_call(

time: 68.1 us -> 67.4 us (0.990)
  transfers between devices with their start and end apart: 3 -> 3, of which waited for: 1 -> 0; matrix products, arithmetic and copies ran while one was open for 0% -> 0% of each run, Pallas kernels for 3% -> 3%
where the time goes in v4:
time: 67.4 us; the launch traced here: 67 us
  blocking collectives  41.4 us (61%)
  starting transfers between devices  13.9 us (21%)
  Pallas kernels  8.8 us (13%)
  local copies, waits for them, and re-layouts  2.69 us (4%)
    all_gather x1, blocking collectives, shards(): kv = lax.all_gather(kv, 'yh', axis=0, tiled=True)  19.4 us
    all_gather x1, blocking collectives, shards(): cores = lax.all_gather(send, 'core', axis=0, tiled=False)  9.38 us
    all_gather x1, blocking collectives, shards(): other = lax.all_gather(other, 'zl', axis=0, tiled=False)  7.49 us
    ppermute x1, starting transfers between devices, shards(): lax.ppermute(stream[0], 'section', [(i, (i + 1) % sections) for i in rang...  5.48 us
    all_gather x1, blocking collectives, shards(): pair = lax.all_gather(query[0], 'yl', axis=0, tiled=True)  5.19 us
    all_to_all x1, starting transfers between devices, shards(): parts = lax.all_to_all(parts, ('yl', 'x'), 0, 0, tiled=True)  4.31 us
    all_to_all x1, starting transfers between devices, shards(): queries = lax.all_to_all(queries, 'x', 0, 0, tiled=True)  4.15 us
    pallas_call x1, Pallas kernels, shards(): pl.pallas_call(attend_kernel, in_specs=[smem, vmem, vmem], out_specs=hbm,...  3.73 us
  transfers between devices with their start and end apart: 3, of which 0 were waited for; matrix products, arithmetic and copies ran while one was open for 0% of the time, Pallas kernels for 3%

profile of v4, /device:TPU:1, one launch (start us, length us, event | category | flops | bytes accessed | tf_op | source)
XLA Modules:
  0.0 67.0 jit_solution(1445201694607244538)
XLA Ops:
  0.0 5.2 %all-gather = bf16[1,256,384]{2,1,0:T(8,128)(2,1)S(1)} all-gather(bf16[1,128,384]{2,1,0:T(8,128)(2,1)} %param.12), channel_id=2, replica_groups=mesh['section'=4,'x'=4,'yh'=4,'yl'=2,'zl'=2,'core'=2] {'yl'}, dimensions={1}, use_global_device_ids=true | all-gather | bytes 294912 | tf_op jit(solution)/shard_map/all_gather | solution.py:195
  5.2 0.9 %shard_map.100 = bf16[4,256,384]{2,1,0:T(8,128)(2,1)} custom-call(bf16[256,384]{1,0:T(8,128)(2,1)S(1)} %bitcast.19), custom_call_target="tpu_custom_call" | custom-call | tf_op jit(solution)/shard_map/pallas_call | solution.py:196
  6.2 4.1 %all-to-all-start = ((bf16[4,256,384]{2,1,0:T(8,128)(2,1)}), bf16[4,256,384]{2,1,0:T(8,128)(2,1)S(1)}, u32[]{:S(2)}, u32[]{:S(2)}) async-start(bf16[4,256,384]{2,1,0:T(8,128)(2,1)} %shard_map.100), calls=%async_computation | async-start | bytes 1572864 | tf_op jit(solution)/shard_map/all_to_all | solution.py:205
  10.3 0.0 copy-done.6
  10.3 0.0 copy-start.5
  10.3 19.4 %all_gather.19.kv_ref = bf16[512,768]{1,0:T(8,128)(2,1)S(1)} all-gather(bf16[128,768]{1,0:T(8,128)(2,1)S(1)} %pad_maximum_fusion), channel_id=1, replica_groups=mesh['section'=4,'x'=4,'yh'=4,'yl'=2,'zl'=2,'core'=2] {'yh'}, dimensions={0}, use_global_device_ids=true | all-gather | bytes 983040 | tf_op jit(solution)/shard_map/all_gather | solution.py:206
  29.7 0.0 all-to-all-done
  29.7 3.7 %shard_map.101 = bf16[8,400,128]{2,1,0:T(8,128)(2,1)} custom-call(s32[4]{0:T(128)S(1)} %copy-done.4, bf16[1024,384]{1,0:T(8,128)(2,1)S(1)} %bitcast.15, bf16[512,768]{1,0:T(8,128)(2,1)S(1)} %all_gather.19.kv_ref), custom_call_target="tpu_custom_call" | custom-call | tf_op jit(solution)/shard_map/pallas_call | solution.py:209
  33.5 4.3 %all-to-all-start.1 = ((bf16[8,400,128]{2,1,0:T(8,128)(2,1)}), bf16[8,400,128]{2,1,0:T(8,128)(2,1)S(1)}, u32[]{:S(2)}, u32[]{:S(2)}) async-start(bf16[8,400,128]{2,1,0:T(8,128)(2,1)} %shard_map.101), calls=%async_computation.1 | async-start | bytes 1638400 | tf_op jit(solution)/shard_map/all_to_all | solution.py:221
  37.8 5.5 %collective-permute-start = (bf16[128,768]{1,0:T(8,128)(2,1)}, bf16[128,768]{1,0:T(8,128)(2,1)}, u32[]{:S(2)}, u32[]{:S(2)}) collective-permute-start(bf16[128,768]{1,0:T(8,128)(2,1)} %bitcast.9), channel_id=1, source_target_pairs={{0,128},{128,256},{256,384},{384,0},{1,129},{129,257},{257,385},{3... | collective-permute-start | bytes 589832 | tf_op jit(solution)/shard_map/ppermute | solution.py:193
  43.3 0.0 copy-start
  43.3 1.7 %copy-done = bf16[1,384,3072]{2,1,0:T(8,128)(2,1)S(1)} copy-done((bf16[1,384,3072]{2,1,0:T(8,128)(2,1)S(1)}, bf16[1,384,3072]{2,1,0:T(8,128)(2,1)}, u32[]{:S(2)}) %copy-start) | copy-done | bytes 2359320
  44.9 1.0 %copy-done.2 = bf16[1,8,384,64]{2,3,1,0:T(8,128)(2,1)S(1)} copy-done((bf16[1,8,384,64]{2,3,1,0:T(8,128)(2,1)S(1)}, bf16[1,8,384,64]{2,3,1,0:T(8,128)(2,1)}, u32[]{:S(2)}) %copy-start.2) | copy-done | bytes 393240
  45.9 0.7 %shard_map.102 = (bf16[384,3072]{1,0:T(8,128)(2,1)S(1)}, bf16[4,64,384]{2,1,0:T(8,128)(2,1)S(1)}) custom-call(s32[4]{0:T(128)S(1)} %copy-done.5, bf16[384,3072]{1,0:T(8,128)(2,1)S(1)} %bitcast.16, bf16[8,64,384]{2,1,0:T(8,128)(2,1)S(1)} %bitcast.20), custom_call_target="tpu_custom_call" | custom-call | tf_op jit(solution)/shard_map/pallas_call | solution.py:224
  46.6 0.0 all-to-all-done.1.part_ref
  46.7 1.4 %shard_map.103 = (bf16[128,1664]{1,0:T(8,128)(2,1)S(1)}, f32[128,1664]{1,0:T(8,128)S(1)}) custom-call(s32[4]{0:T(128)S(1)} %copy-done.4, bf16[8,400,128]{2,1,0:T(8,128)(2,1)S(1)} %all-to-all-done.1.part_ref, bf16[4,64,384]{2,1,0:T(8,128)(2,1)S(1)} %get-tuple-element.11.down_ref, bf16[384,3072]{1,0:T(8,128)(2,1)S(1)} %get-tuple-element.12.w_ref), custom_call_target="tpu_custom_call" | custom-call | tf_op jit(solution)/shard_map/pallas_call | solution.py:235
  48.1 0.0 copy-start.1
  48.1 0.0 copy-start.3
  48.1 9.4 %all-gather.1 = bf16[256,1664]{1,0:T(8,128)(2,1)S(1)} all-gather(bf16[128,1664]{1,0:T(8,128)(2,1)S(1)} %get-tuple-element.14), channel_id=3, replica_groups=mesh['section'=4,'x'=4,'yh'=4,'yl'=2,'zl'=2,'core'=2] {'core'}, dimensions={0}, use_global_device_ids=true | all-gather | bytes 1277952 | tf_op jit(solution)/shard_map/all_gather | solution.py:242
  57.5 0.1 shard_map.104
  57.6 7.5 %all-gather.2 = bf16[256,896]{1,0:T(8,128)(2,1)S(1)} all-gather(bf16[128,896]{1,0:T(8,128)(2,1)S(1)} %get-tuple-element.16), channel_id=4, replica_groups=mesh['section'=4,'x'=4,'yh'=4,'yl'=2,'zl'=2,'core'=2] {'zl'}, dimensions={0}, use_global_device_ids=true | all-gather | bytes 688128 | tf_op jit(solution)/shard_map/all_gather | solution.py:250
  65.1 0.0 collective-permute-done.state_ref
  65.1 0.0 copy-done.1
  65.1 1.9 %shard_map.105 = bf16[128,768]{1,0:T(8,128)(2,1)} custom-call(s32[4]{0:T(128)S(1)} %copy-done.4, s32[4]{0:T(128)S(1)} %copy-done.5, f32[128,896]{1,0:T(8,128)S(1)} %get-tuple-element.15.mine_ref, bf16[2,128,896]{2,1,0:T(8,128)(2,1)S(1)} %bitcast.17, bf16[128,768]{1,0:T(8,128)(2,1)} %collective-permute-done.state_ref, f32[4,768]{1,0:T(4,128)S(1)} %bitcast.21, ...), custom_call_target="tpu_custom_call" | custom-call | tf_op jit(solution)/shard_map/pallas_call | solution.py:252
  (9 shorter events, 0.0 us)
Async XLA Ops:
  0.0 10.3 %copy-start.6 = (bf16[1,128,384]{2,1,0:T(8,128)(2,1)S(1)}, bf16[1,128,384]{2,1,0:T(8,128)(2,1)}, u32[]{:S(2)}) copy-start(bf16[1,128,384]{2,1,0:T(8,128)(2,1)} %param.14) | copy-start | bytes 294916
  0.0 10.3 %copy-start.7 = (bf16[1,128,384]{2,1,0:T(8,128)(2,1)S(1)}, bf16[1,128,384]{2,1,0:T(8,128)(2,1)}, u32[]{:S(2)}) copy-start(bf16[1,128,384]{2,1,0:T(8,128)(2,1)} %param.13) | copy-start | bytes 294916
  0.0 29.7 %copy-start.4 = (s32[4]{0:T(128)S(1)}, s32[4]{0:T(128)}, u32[]{:S(2)}) copy-start(s32[4]{0:T(128)} %lengths_ref.5) | copy-start | bytes 52
  6.2 23.6 %all-to-all-start = ((bf16[4,256,384]{2,1,0:T(8,128)(2,1)}), bf16[4,256,384]{2,1,0:T(8,128)(2,1)S(1)}, u32[]{:S(2)}, u32[]{:S(2)}) async-start(bf16[4,256,384]{2,1,0:T(8,128)(2,1)} %shard_map.100), calls=%async_computation | async-start | bytes 1572864 | tf_op jit(solution)/shard_map/all_to_all | solution.py:205
  10.3 32.9 %copy-start.5 = (s32[4]{0:T(128)S(1)}, s32[4]{0:T(128)}, u32[]{:S(2)}) copy-start(s32[4]{0:T(128)} %adapter_ref.3) | copy-start | bytes 52
  33.5 13.2 %all-to-all-start.1 = ((bf16[8,400,128]{2,1,0:T(8,128)(2,1)}), bf16[8,400,128]{2,1,0:T(8,128)(2,1)S(1)}, u32[]{:S(2)}, u32[]{:S(2)}) async-start(bf16[8,400,128]{2,1,0:T(8,128)(2,1)} %shard_map.101), calls=%async_computation.1 | async-start | bytes 1638400 | tf_op jit(solution)/shard_map/all_to_all | solution.py:221
  37.8 27.3 %collective-permute-start = (bf16[128,768]{1,0:T(8,128)(2,1)}, bf16[128,768]{1,0:T(8,128)(2,1)}, u32[]{:S(2)}, u32[]{:S(2)}) collective-permute-start(bf16[128,768]{1,0:T(8,128)(2,1)} %bitcast.9), channel_id=1, source_target_pairs={{0,128},{128,256},{256,384},{384,0},{1,129},{129,257},{257,385},{3... | collective-permute-start | bytes 589832 | tf_op jit(solution)/shard_map/ppermute | solution.py:193
  43.3 1.7 %copy-start = (bf16[1,384,3072]{2,1,0:T(8,128)(2,1)S(1)}, bf16[1,384,3072]{2,1,0:T(8,128)(2,1)}, u32[]{:S(2)}) copy-start(bf16[1,384,3072]{2,1,0:T(8,128)(2,1)} %param.17) | copy-start | bytes 7077892
  44.9 1.0 %copy-start.2 = (bf16[1,8,384,64]{2,3,1,0:T(8,128)(2,1)S(1)}, bf16[1,8,384,64]{2,3,1,0:T(8,128)(2,1)}, u32[]{:S(2)}) copy-start(bf16[1,8,384,64]{2,3,1,0:T(8,128)(2,1)} %param.18) | copy-start | bytes 1179652
  48.1 17.0 %copy-start.1 = (bf16[1,8,64,768]{3,2,1,0:T(8,128)(2,1)S(1)}, bf16[1,8,64,768]{3,2,1,0:T(8,128)(2,1)}, u32[]{:S(2)}) copy-start(bf16[1,8,64,768]{3,2,1,0:T(8,128)(2,1)} %param.19) | copy-start | bytes 2359300
  48.1 17.0 %copy-start.3 = (f32[1,4,768]{2,1,0:T(4,128)S(1)}, f32[1,4,768]{2,1,0:T(4,128)}, u32[]{:S(2)}) copy-start(f32[1,4,768]{2,1,0:T(4,128)} %param.16) | copy-start | bytes 36868

commit v5 on v4

--- a/solution.py
+++ b/solution.py
@@ -13,9 +13,10 @@
 NX, NYH, NYL = 4, 4, 2
 NZ, NC = 2, 2
 STAT_ROWS = 16
+ORDER = [0, 4, 2, 6, 1, 5, 3, 7]
 F32 = jnp.float32
 BF16 = jnp.bfloat16
-VMEM_LIMIT = 32 * 1024 * 1024
+VMEM_LIMIT = 16 * 1024 * 1024
 
 
 def segment_of(position, lengths_ref):
@@ -93,7 +94,7 @@
         part = jnp.dot(vt_ref[h * HEAD : (h + 1) * HEAD, :], weight.astype(BF16), preferred_element_type=F32)
         part = (part * (1.0 / total)).astype(BF16)
         for i in range(blocks):
-            out_ref[(i % NYL) * NX + i // NYL, h * HEAD : (h + 1) * HEAD, :] = part[:, i * rows : (i + 1) * rows]
+            out_ref[ORDER.index(i), h * HEAD : (h + 1) * HEAD, :] = part[:, i * rows : (i + 1) * rows]
         send(h * HEAD, HEAD)
         level = top * scale + jnp.log2(total)
         a = level.astype(BF16).astype(F32)
@@ -104,7 +105,7 @@
     blank = [jnp.zeros((1, n_q), F32)] * (STAT_ROWS - 3 * heads)
     stats = jnp.concatenate(high + mid + low + blank, axis=0).astype(BF16)
     for i in range(blocks):
-        out_ref[(i % NYL) * NX + i // NYL, feats : feats + STAT_ROWS, :] = stats[:, i * rows : (i + 1) * rows]
+        out_ref[ORDER.index(i), feats : feats + STAT_ROWS, :] = stats[:, i * rows : (i + 1) * rows]
     send(feats, STAT_ROWS)
     for copy in copies:
         copy.wait()
@@ -144,8 +145,11 @@
     keep_ref[:, NZ * quarter : NZ * quarter + HEAD] = rank.astype(keep_ref.dtype)
 
 
-def hold_kernel(adapter_ref, matrix_ref, down_ref, w_ref, chosen_ref):
+def hold_kernel(matrix_ref, w_ref):
     w_ref[...] = matrix_ref[...]
+
+
+def choose_kernel(adapter_ref, down_ref, chosen_ref):
     for r in range(chosen_ref.shape[0]):
         chosen_ref[r] = down_ref[adapter_ref[r]]
 
@@ -218,19 +222,23 @@
         ],
         compiler_params=params,
     )(lengths, queries.reshape(group * rows, feats), kv)
-    parts = lax.all_to_all(parts, ("yl", "x"), 0, 0, tiled=True)
+    parts = lax.all_to_all(parts, ("x", "yl"), 0, 0, tiled=True, axis_index_groups=[ORDER])
 
     down = jnp.swapaxes(adapter_down[0], 1, 2)
-    matrix, down = pl.pallas_call(
+    matrix = pl.pallas_call(
         hold_kernel,
-        in_specs=[smem, vmem, vmem],
-        out_specs=[vmem, vmem],
-        out_shape=[
-            jax.ShapeDtypeStruct(output_matrix.shape[1:], BF16),
-            jax.ShapeDtypeStruct((adapter.shape[0],) + down.shape[1:], BF16),
-        ],
-        compiler_params=pltpu.CompilerParams(vmem_limit_bytes=VMEM_LIMIT),
-    )(adapter, output_matrix[0], down)
+        in_specs=[vmem],
+        out_specs=vmem,
+        out_shape=jax.ShapeDtypeStruct(output_matrix.shape[1:], BF16),
+        compiler_params=params,
+    )(output_matrix[0])
+    down = pl.pallas_call(
+        choose_kernel,
+        in_specs=[smem, vmem],
+        out_specs=vmem,
+        out_shape=jax.ShapeDtypeStruct((adapter.shape[0],) + down.shape[1:], BF16),
+        compiler_params=params,
+    )(adapter, down)
     width = NZ * quarter + HEAD
     send, keep = pl.pallas_call(
         project_kernel,

time: 67.4 us -> 67.1 us (level)
  no operation moved by 1% of the time
where the time goes in v5:
time: 67.1 us; the launch traced here: 66.7 us
  blocking collectives  41.3 us (62%)
  starting transfers between devices  14 us (21%)
  Pallas kernels  8.81 us (13%)
  local copies, waits for them, and re-layouts  2.53 us (4%)
    all_gather x1, blocking collectives, shards(): kv = lax.all_gather(kv, 'yh', axis=0, tiled=True)  19.4 us
    all_gather x1, blocking collectives, shards(): cores = lax.all_gather(send, 'core', axis=0, tiled=False)  9.26 us
    all_gather x1, blocking collectives, shards(): other = lax.all_gather(other, 'zl', axis=0, tiled=False)  7.49 us
    ppermute x1, starting transfers between devices, shards(): lax.ppermute(stream[0], 'section', [(i, (i + 1) % sections) for i in rang...  5.5 us
    all_gather x1, blocking collectives, shards(): pair = lax.all_gather(query[0], 'yl', axis=0, tiled=True)  5.19 us
    all_to_all x1, starting transfers between devices, shards(): lax.all_to_all(parts, ('x', 'yl'), 0, 0, tiled=True, axis_index_groups=[O...  4.31 us
    all_to_all x1, starting transfers between devices, shards(): queries = lax.all_to_all(queries, 'x', 0, 0, tiled=True)  4.15 us
    pallas_call x1, Pallas kernels, shards(): pl.pallas_call(attend_kernel, in_specs=[smem, vmem, vmem], out_specs=hbm,...  3.74 us
  transfers between devices with their start and end apart: 3, of which 0 were waited for; matrix products, arithmetic and copies ran while one was open for 0% of the time, Pallas kernels for 3%

profile of v5, /device:TPU:1, one launch (start us, length us, event | category | flops | bytes accessed | tf_op | source)
XLA Modules:
  0.0 66.7 jit_solution(1750541174988227881)
XLA Ops:
  0.0 5.2 %all-gather = bf16[1,256,384]{2,1,0:T(8,128)(2,1)S(1)} all-gather(bf16[1,128,384]{2,1,0:T(8,128)(2,1)} %param.12), channel_id=2, replica_groups=mesh['section'=4,'x'=4,'yh'=4,'yl'=2,'zl'=2,'core'=2] {'yl'}, dimensions={1}, use_global_device_ids=true | all-gather | bytes 294912 | tf_op jit(solution)/shard_map/all_gather | solution.py:199
  5.2 0.9 %shard_map.100 = bf16[4,256,384]{2,1,0:T(8,128)(2,1)} custom-call(bf16[256,384]{1,0:T(8,128)(2,1)S(1)} %bitcast.19), custom_call_target="tpu_custom_call" | custom-call | tf_op jit(solution)/shard_map/pallas_call | solution.py:200
  6.2 4.1 %all-to-all-start = ((bf16[4,256,384]{2,1,0:T(8,128)(2,1)}), bf16[4,256,384]{2,1,0:T(8,128)(2,1)S(1)}, u32[]{:S(2)}, u32[]{:S(2)}) async-start(bf16[4,256,384]{2,1,0:T(8,128)(2,1)} %shard_map.100), calls=%async_computation | async-start | bytes 1572864 | tf_op jit(solution)/shard_map/all_to_all | solution.py:209
  10.3 0.0 copy-done.7
  10.3 0.0 copy-done.6
  10.3 19.4 %all_gather.19.kv_ref = bf16[512,768]{1,0:T(8,128)(2,1)S(1)} all-gather(bf16[128,768]{1,0:T(8,128)(2,1)S(1)} %pad_maximum_fusion), channel_id=1, replica_groups=mesh['section'=4,'x'=4,'yh'=4,'yl'=2,'zl'=2,'core'=2] {'yh'}, dimensions={0}, use_global_device_ids=true | all-gather | bytes 983040 | tf_op jit(solution)/shard_map/all_gather | solution.py:210
  29.7 0.0 all-to-all-done
  29.7 3.7 %shard_map.101 = bf16[8,400,128]{2,1,0:T(8,128)(2,1)} custom-call(s32[4]{0:T(128)S(1)} %copy-done.4, bf16[1024,384]{1,0:T(8,128)(2,1)S(1)} %bitcast.15, bf16[512,768]{1,0:T(8,128)(2,1)S(1)} %all_gather.19.kv_ref), custom_call_target="tpu_custom_call" | custom-call | tf_op jit(solution)/shard_map/pallas_call | solution.py:213
  33.5 4.3 %all-to-all-start.1 = ((bf16[8,400,128]{2,1,0:T(8,128)(2,1)}), bf16[8,400,128]{2,1,0:T(8,128)(2,1)S(1)}, u32[]{:S(2)}, u32[]{:S(2)}) async-start(bf16[8,400,128]{2,1,0:T(8,128)(2,1)} %shard_map.101), calls=%async_computation.1 | async-start | bytes 1638400 | tf_op jit(solution)/shard_map/all_to_all | solution.py:225
  37.8 5.5 %collective-permute-start = (bf16[128,768]{1,0:T(8,128)(2,1)}, bf16[128,768]{1,0:T(8,128)(2,1)}, u32[]{:S(2)}, u32[]{:S(2)}) collective-permute-start(bf16[128,768]{1,0:T(8,128)(2,1)} %bitcast.9), channel_id=1, source_target_pairs={{0,128},{128,256},{256,384},{384,0},{1,129},{129,257},{257,385},{3... | collective-permute-start | bytes 589832 | tf_op jit(solution)/shard_map/ppermute | solution.py:197
  43.3 0.0 copy-start
  43.3 1.7 %copy-done = bf16[1,384,3072]{2,1,0:T(8,128)(2,1)S(1)} copy-done((bf16[1,384,3072]{2,1,0:T(8,128)(2,1)S(1)}, bf16[1,384,3072]{2,1,0:T(8,128)(2,1)}, u32[]{:S(2)}) %copy-start) | copy-done | bytes 2359320
  44.9 0.2 shard_map.103.w_ref
  45.1 0.8 %copy-done.2 = bf16[1,8,384,64]{2,3,1,0:T(8,128)(2,1)S(1)} copy-done((bf16[1,8,384,64]{2,3,1,0:T(8,128)(2,1)S(1)}, bf16[1,8,384,64]{2,3,1,0:T(8,128)(2,1)}, u32[]{:S(2)}) %copy-start.2) | copy-done | bytes 393240
  45.9 0.6 shard_map.102.down_ref
  46.5 0.0 all-to-all-done.1.part_ref
  46.5 1.4 %shard_map.104 = (bf16[128,1664]{1,0:T(8,128)(2,1)S(1)}, f32[128,1664]{1,0:T(8,128)S(1)}) custom-call(s32[4]{0:T(128)S(1)} %copy-done.4, bf16[8,400,128]{2,1,0:T(8,128)(2,1)S(1)} %all-to-all-done.1.part_ref, bf16[4,64,384]{2,1,0:T(8,128)(2,1)S(1)} %shard_map.102.down_ref, bf16[384,3072]{1,0:T(8,128)(2,1)S(1)} %shard_map.103.w_ref), custom_call_target="tpu_custom_call" | custom-call | tf_op jit(solution)/shard_map/pallas_call | solution.py:243
  48.0 0.0 copy-start.1
  48.0 0.0 copy-start.3
  48.0 9.3 %all-gather.1 = bf16[256,1664]{1,0:T(8,128)(2,1)S(1)} all-gather(bf16[128,1664]{1,0:T(8,128)(2,1)S(1)} %get-tuple-element.10), channel_id=3, replica_groups=mesh['section'=4,'x'=4,'yh'=4,'yl'=2,'zl'=2,'core'=2] {'core'}, dimensions={0}, use_global_device_ids=true | all-gather | bytes 1277952 | tf_op jit(solution)/shard_map/all_gather | solution.py:250
  57.3 0.1 shard_map.105
  57.3 7.5 %all-gather.2 = bf16[256,896]{1,0:T(8,128)(2,1)S(1)} all-gather(bf16[128,896]{1,0:T(8,128)(2,1)S(1)} %get-tuple-element.12), channel_id=4, replica_groups=mesh['section'=4,'x'=4,'yh'=4,'yl'=2,'zl'=2,'core'=2] {'zl'}, dimensions={0}, use_global_device_ids=true | all-gather | bytes 688128 | tf_op jit(solution)/shard_map/all_gather | solution.py:258
  64.8 0.0 collective-permute-done.state_ref
  64.9 1.9 %shard_map.106 = bf16[128,768]{1,0:T(8,128)(2,1)} custom-call(s32[4]{0:T(128)S(1)} %copy-done.4, s32[4]{0:T(128)S(1)} %copy-done.5, f32[128,896]{1,0:T(8,128)S(1)} %get-tuple-element.11.mine_ref, bf16[2,128,896]{2,1,0:T(8,128)(2,1)S(1)} %bitcast.17, bf16[128,768]{1,0:T(8,128)(2,1)} %collective-permute-done.state_ref, f32[4,768]{1,0:T(4,128)S(1)} %bitcast.21, ...), custom_call_target="tpu_custom_call" | custom-call | tf_op jit(solution)/shard_map/pallas_call | solution.py:260
  (10 shorter events, 0.0 us)
Async XLA Ops:
  0.0 10.3 %copy-start.7 = (bf16[1,128,384]{2,1,0:T(8,128)(2,1)S(1)}, bf16[1,128,384]{2,1,0:T(8,128)(2,1)}, u32[]{:S(2)}) copy-start(bf16[1,128,384]{2,1,0:T(8,128)(2,1)} %param.13) | copy-start | bytes 294916
  0.0 10.3 %copy-start.6 = (bf16[1,128,384]{2,1,0:T(8,128)(2,1)S(1)}, bf16[1,128,384]{2,1,0:T(8,128)(2,1)}, u32[]{:S(2)}) copy-start(bf16[1,128,384]{2,1,0:T(8,128)(2,1)} %param.14) | copy-start | bytes 294916
  0.0 29.7 %copy-start.4 = (s32[4]{0:T(128)S(1)}, s32[4]{0:T(128)}, u32[]{:S(2)}) copy-start(s32[4]{0:T(128)} %lengths_ref.5) | copy-start | bytes 52
  6.2 23.5 %all-to-all-start = ((bf16[4,256,384]{2,1,0:T(8,128)(2,1)}), bf16[4,256,384]{2,1,0:T(8,128)(2,1)S(1)}, u32[]{:S(2)}, u32[]{:S(2)}) async-start(bf16[4,256,384]{2,1,0:T(8,128)(2,1)} %shard_map.100), calls=%async_computation | async-start | bytes 1572864 | tf_op jit(solution)/shard_map/all_to_all | solution.py:209
  33.5 13.1 %all-to-all-start.1 = ((bf16[8,400,128]{2,1,0:T(8,128)(2,1)}), bf16[8,400,128]{2,1,0:T(8,128)(2,1)S(1)}, u32[]{:S(2)}, u32[]{:S(2)}) async-start(bf16[8,400,128]{2,1,0:T(8,128)(2,1)} %shard_map.101), calls=%async_computation.1 | async-start | bytes 1638400 | tf_op jit(solution)/shard_map/all_to_all | solution.py:225
  37.8 27.1 %collective-permute-start = (bf16[128,768]{1,0:T(8,128)(2,1)}, bf16[128,768]{1,0:T(8,128)(2,1)}, u32[]{:S(2)}, u32[]{:S(2)}) collective-permute-start(bf16[128,768]{1,0:T(8,128)(2,1)} %bitcast.9), channel_id=1, source_target_pairs={{0,128},{128,256},{256,384},{384,0},{1,129},{129,257},{257,385},{3... | collective-permute-start | bytes 589832 | tf_op jit(solution)/shard_map/ppermute | solution.py:197
  43.3 1.7 %copy-start = (bf16[1,384,3072]{2,1,0:T(8,128)(2,1)S(1)}, bf16[1,384,3072]{2,1,0:T(8,128)(2,1)}, u32[]{:S(2)}) copy-start(bf16[1,384,3072]{2,1,0:T(8,128)(2,1)} %param.17) | copy-start | bytes 7077892
  44.9 1.0 %copy-start.2 = (bf16[1,8,384,64]{2,3,1,0:T(8,128)(2,1)S(1)}, bf16[1,8,384,64]{2,3,1,0:T(8,128)(2,1)}, u32[]{:S(2)}) copy-start(bf16[1,8,384,64]{2,3,1,0:T(8,128)(2,1)} %param.18) | copy-start | bytes 1179652
  44.9 1.0 %copy-start.5 = (s32[4]{0:T(128)S(1)}, s32[4]{0:T(128)}, u32[]{:S(2)}) copy-start(s32[4]{0:T(128)} %adapter_ref.3) | copy-start | bytes 52
  48.0 16.9 %copy-start.1 = (bf16[1,8,64,768]{3,2,1,0:T(8,128)(2,1)S(1)}, bf16[1,8,64,768]{3,2,1,0:T(8,128)(2,1)}, u32[]{:S(2)}) copy-start(bf16[1,8,64,768]{3,2,1,0:T(8,128)(2,1)} %param.19) | copy-start | bytes 2359300
  48.0 16.9 %copy-start.3 = (f32[1,4,768]{2,1,0:T(4,128)S(1)}, f32[1,4,768]{2,1,0:T(4,128)}, u32[]{:S(2)}) copy-start(f32[1,4,768]{2,1,0:T(4,128)} %param.16) | copy-start | bytes 36868

commit v6 on v5

--- a/solution.py
+++ b/solution.py
@@ -162,7 +162,7 @@
             (pl.ds(pl.multiple_of(which * quarter, quarter), quarter), pl.ds(0, quarter)),
             (pl.ds(NZ * quarter, HEAD), pl.ds(quarter, HEAD)),
         ):
-            ref[:, at] = (keep_ref[:, cols] + cores_ref[1 - core, :, cols].astype(F32)).astype(ref.dtype)
+            ref[:, at] = (keep_ref[:, cols].astype(F32) + cores_ref[1 - core, :, cols].astype(F32)).astype(ref.dtype)
 
 
 def finish_kernel(lengths_ref, adapter_ref, mine_ref, other_ref, state_ref, gate_ref, up_ref, out_ref):
@@ -244,7 +244,7 @@
         project_kernel,
         in_specs=[smem, vmem, vmem, vmem],
         out_specs=[vmem, vmem],
-        out_shape=[jax.ShapeDtypeStruct((rows, width), BF16), jax.ShapeDtypeStruct((rows, width), F32)],
+        out_shape=[jax.ShapeDtypeStruct((rows, width), BF16), jax.ShapeDtypeStruct((rows, width), BF16)],
         compiler_params=params,
     )(lengths, parts, down, matrix)
     cores = lax.all_gather(send, "core", axis=0, tiled=False)

time: 67.1 us -> 67.1 us (level)
  no operation moved by 1% of the time
where the time goes in v6:
time: 67.1 us; the launch traced here: 66.8 us
  blocking collectives  41.3 us (62%)
  starting transfers between devices  14 us (21%)
  Pallas kernels  8.82 us (13%)
  local copies, waits for them, and re-layouts  2.53 us (4%)
    all_gather x1, blocking collectives, shards(): kv = lax.all_gather(kv, 'yh', axis=0, tiled=True)  19.4 us
    all_gather x1, blocking collectives, shards(): cores = lax.all_gather(send, 'core', axis=0, tiled=False)  9.26 us
    all_gather x1, blocking collectives, shards(): other = lax.all_gather(other, 'zl', axis=0, tiled=False)  7.49 us
    ppermute x1, starting transfers between devices, shards(): lax.ppermute(stream[0], 'section', [(i, (i + 1) % sections) for i in rang...  5.5 us
    all_gather x1, blocking collectives, shards(): pair = lax.all_gather(query[0], 'yl', axis=0, tiled=True)  5.19 us
    all_to_all x1, starting transfers between devices, shards(): lax.all_to_all(parts, ('x', 'yl'), 0, 0, tiled=True, axis_index_groups=[O...  4.31 us
    all_to_all x1, starting transfers between devices, shards(): queries = lax.all_to_all(queries, 'x', 0, 0, tiled=True)  4.15 us
    pallas_call x1, Pallas kernels, shards(): pl.pallas_call(attend_kernel, in_specs=[smem, vmem, vmem], out_specs=hbm,...  3.74 us
  transfers between devices with their start and end apart: 3, of which 0 were waited for; matrix products, arithmetic and copies ran while one was open for 0% of the time, Pallas kernels for 3%

profile of v6, /device:TPU:1, one launch (start us, length us, event | category | flops | bytes accessed | tf_op | source)
XLA Modules:
  0.0 66.8 jit_solution(16328035891859973268)
XLA Ops:
  0.0 5.2 %all-gather = bf16[1,256,384]{2,1,0:T(8,128)(2,1)S(1)} all-gather(bf16[1,128,384]{2,1,0:T(8,128)(2,1)} %param.12), channel_id=2, replica_groups=mesh['section'=4,'x'=4,'yh'=4,'yl'=2,'zl'=2,'core'=2] {'yl'}, dimensions={1}, use_global_device_ids=true | all-gather | bytes 294912 | tf_op jit(solution)/shard_map/all_gather | solution.py:199
  5.2 0.9 %shard_map.100 = bf16[4,256,384]{2,1,0:T(8,128)(2,1)} custom-call(bf16[256,384]{1,0:T(8,128)(2,1)S(1)} %bitcast.19), custom_call_target="tpu_custom_call" | custom-call | tf_op jit(solution)/shard_map/pallas_call | solution.py:200
  6.2 4.1 %all-to-all-start = ((bf16[4,256,384]{2,1,0:T(8,128)(2,1)}), bf16[4,256,384]{2,1,0:T(8,128)(2,1)S(1)}, u32[]{:S(2)}, u32[]{:S(2)}) async-start(bf16[4,256,384]{2,1,0:T(8,128)(2,1)} %shard_map.100), calls=%async_computation | async-start | bytes 1572864 | tf_op jit(solution)/shard_map/all_to_all | solution.py:209
  10.3 0.0 copy-done.7
  10.3 19.4 %all_gather.19.kv_ref = bf16[512,768]{1,0:T(8,128)(2,1)S(1)} all-gather(bf16[128,768]{1,0:T(8,128)(2,1)S(1)} %pad_maximum_fusion), channel_id=1, replica_groups=mesh['section'=4,'x'=4,'yh'=4,'yl'=2,'zl'=2,'core'=2] {'yh'}, dimensions={0}, use_global_device_ids=true | all-gather | bytes 983040 | tf_op jit(solution)/shard_map/all_gather | solution.py:210
  29.7 0.0 all-to-all-done
  29.7 3.7 %shard_map.101 = bf16[8,400,128]{2,1,0:T(8,128)(2,1)} custom-call(s32[4]{0:T(128)S(1)} %copy-done.4, bf16[1024,384]{1,0:T(8,128)(2,1)S(1)} %bitcast.15, bf16[512,768]{1,0:T(8,128)(2,1)S(1)} %all_gather.19.kv_ref), custom_call_target="tpu_custom_call" | custom-call | tf_op jit(solution)/shard_map/pallas_call | solution.py:213
  33.5 4.3 %all-to-all-start.1 = ((bf16[8,400,128]{2,1,0:T(8,128)(2,1)}), bf16[8,400,128]{2,1,0:T(8,128)(2,1)S(1)}, u32[]{:S(2)}, u32[]{:S(2)}) async-start(bf16[8,400,128]{2,1,0:T(8,128)(2,1)} %shard_map.101), calls=%async_computation.1 | async-start | bytes 1638400 | tf_op jit(solution)/shard_map/all_to_all | solution.py:225
  37.8 5.5 %collective-permute-start = (bf16[128,768]{1,0:T(8,128)(2,1)}, bf16[128,768]{1,0:T(8,128)(2,1)}, u32[]{:S(2)}, u32[]{:S(2)}) collective-permute-start(bf16[128,768]{1,0:T(8,128)(2,1)} %bitcast.9), channel_id=1, source_target_pairs={{0,128},{128,256},{256,384},{384,0},{1,129},{129,257},{257,385},{3... | collective-permute-start | bytes 589832 | tf_op jit(solution)/shard_map/ppermute | solution.py:197
  43.3 0.0 copy-start
  43.3 1.7 %copy-done = bf16[1,384,3072]{2,1,0:T(8,128)(2,1)S(1)} copy-done((bf16[1,384,3072]{2,1,0:T(8,128)(2,1)S(1)}, bf16[1,384,3072]{2,1,0:T(8,128)(2,1)}, u32[]{:S(2)}) %copy-start) | copy-done | bytes 2359320
  44.9 0.2 shard_map.103.w_ref
  45.1 0.8 %copy-done.2 = bf16[1,8,384,64]{2,3,1,0:T(8,128)(2,1)S(1)} copy-done((bf16[1,8,384,64]{2,3,1,0:T(8,128)(2,1)S(1)}, bf16[1,8,384,64]{2,3,1,0:T(8,128)(2,1)}, u32[]{:S(2)}) %copy-start.2) | copy-done | bytes 393240
  45.9 0.0 copy-done.5
  45.9 0.6 shard_map.102.down_ref
  46.5 0.0 all-to-all-done.1.part_ref
  46.5 1.4 %shard_map.104 = (bf16[128,1664]{1,0:T(8,128)(2,1)S(1)}, bf16[128,1664]{1,0:T(8,128)(2,1)S(1)}) custom-call(s32[4]{0:T(128)S(1)} %copy-done.4, bf16[8,400,128]{2,1,0:T(8,128)(2,1)S(1)} %all-to-all-done.1.part_ref, bf16[4,64,384]{2,1,0:T(8,128)(2,1)S(1)} %shard_map.102.down_ref, bf16[384,3072]{1,0:T(8,128)(2,1)S(1)} %shard_map.103.w_ref), custom_call_target="tpu_custom_call" | custom-call | tf_op jit(solution)/shard_map/pallas_call | solution.py:243
  48.0 0.0 copy-start.1
  48.0 0.0 copy-start.3
  48.0 9.3 %all-gather.1 = bf16[256,1664]{1,0:T(8,128)(2,1)S(1)} all-gather(bf16[128,1664]{1,0:T(8,128)(2,1)S(1)} %get-tuple-element.10), channel_id=3, replica_groups=mesh['section'=4,'x'=4,'yh'=4,'yl'=2,'zl'=2,'core'=2] {'core'}, dimensions={0}, use_global_device_ids=true | all-gather | bytes 1277952 | tf_op jit(solution)/shard_map/all_gather | solution.py:250
  57.3 0.1 shard_map.105
  57.4 7.5 %all-gather.2 = bf16[256,896]{1,0:T(8,128)(2,1)S(1)} all-gather(bf16[128,896]{1,0:T(8,128)(2,1)S(1)} %get-tuple-element.12), channel_id=4, replica_groups=mesh['section'=4,'x'=4,'yh'=4,'yl'=2,'zl'=2,'core'=2] {'zl'}, dimensions={0}, use_global_device_ids=true | all-gather | bytes 688128 | tf_op jit(solution)/shard_map/all_gather | solution.py:258
  64.9 0.0 collective-permute-done.state_ref
  64.9 1.9 %shard_map.106 = bf16[128,768]{1,0:T(8,128)(2,1)} custom-call(s32[4]{0:T(128)S(1)} %copy-done.4, s32[4]{0:T(128)S(1)} %copy-done.5, f32[128,896]{1,0:T(8,128)S(1)} %get-tuple-element.11.mine_ref, bf16[2,128,896]{2,1,0:T(8,128)(2,1)S(1)} %bitcast.17, bf16[128,768]{1,0:T(8,128)(2,1)} %collective-permute-done.state_ref, f32[4,768]{1,0:T(4,128)S(1)} %bitcast.21, ...), custom_call_target="tpu_custom_call" | custom-call | tf_op jit(solution)/shard_map/pallas_call | solution.py:260
  (10 shorter events, 0.0 us)
Async XLA Ops:
  0.0 10.3 %copy-start.7 = (bf16[1,128,384]{2,1,0:T(8,128)(2,1)S(1)}, bf16[1,128,384]{2,1,0:T(8,128)(2,1)}, u32[]{:S(2)}) copy-start(bf16[1,128,384]{2,1,0:T(8,128)(2,1)} %param.13) | copy-start | bytes 294916
  0.0 10.3 %copy-start.6 = (bf16[1,128,384]{2,1,0:T(8,128)(2,1)S(1)}, bf16[1,128,384]{2,1,0:T(8,128)(2,1)}, u32[]{:S(2)}) copy-start(bf16[1,128,384]{2,1,0:T(8,128)(2,1)} %param.14) | copy-start | bytes 294916
  0.0 29.7 %copy-start.4 = (s32[4]{0:T(128)S(1)}, s32[4]{0:T(128)}, u32[]{:S(2)}) copy-start(s32[4]{0:T(128)} %lengths_ref.5) | copy-start | bytes 52
  6.2 23.5 %all-to-all-start = ((bf16[4,256,384]{2,1,0:T(8,128)(2,1)}), bf16[4,256,384]{2,1,0:T(8,128)(2,1)S(1)}, u32[]{:S(2)}, u32[]{:S(2)}) async-start(bf16[4,256,384]{2,1,0:T(8,128)(2,1)} %shard_map.100), calls=%async_computation | async-start | bytes 1572864 | tf_op jit(solution)/shard_map/all_to_all | solution.py:209
  33.5 13.1 %all-to-all-start.1 = ((bf16[8,400,128]{2,1,0:T(8,128)(2,1)}), bf16[8,400,128]{2,1,0:T(8,128)(2,1)S(1)}, u32[]{:S(2)}, u32[]{:S(2)}) async-start(bf16[8,400,128]{2,1,0:T(8,128)(2,1)} %shard_map.101), calls=%async_computation.1 | async-start | bytes 1638400 | tf_op jit(solution)/shard_map/all_to_all | solution.py:225
  37.8 27.1 %collective-permute-start = (bf16[128,768]{1,0:T(8,128)(2,1)}, bf16[128,768]{1,0:T(8,128)(2,1)}, u32[]{:S(2)}, u32[]{:S(2)}) collective-permute-start(bf16[128,768]{1,0:T(8,128)(2,1)} %bitcast.9), channel_id=1, source_target_pairs={{0,128},{128,256},{256,384},{384,0},{1,129},{129,257},{257,385},{3... | collective-permute-start | bytes 589832 | tf_op jit(solution)/shard_map/ppermute | solution.py:197
  43.3 1.7 %copy-start = (bf16[1,384,3072]{2,1,0:T(8,128)(2,1)S(1)}, bf16[1,384,3072]{2,1,0:T(8,128)(2,1)}, u32[]{:S(2)}) copy-start(bf16[1,384,3072]{2,1,0:T(8,128)(2,1)} %param.17) | copy-start | bytes 7077892
  44.9 1.0 %copy-start.2 = (bf16[1,8,384,64]{2,3,1,0:T(8,128)(2,1)S(1)}, bf16[1,8,384,64]{2,3,1,0:T(8,128)(2,1)}, u32[]{:S(2)}) copy-start(bf16[1,8,384,64]{2,3,1,0:T(8,128)(2,1)} %param.18) | copy-start | bytes 1179652
  44.9 1.0 %copy-start.5 = (s32[4]{0:T(128)S(1)}, s32[4]{0:T(128)}, u32[]{:S(2)}) copy-start(s32[4]{0:T(128)} %adapter_ref.3) | copy-start | bytes 52
  48.0 16.9 %copy-start.1 = (bf16[1,8,64,768]{3,2,1,0:T(8,128)(2,1)S(1)}, bf16[1,8,64,768]{3,2,1,0:T(8,128)(2,1)}, u32[]{:S(2)}) copy-start(bf16[1,8,64,768]{3,2,1,0:T(8,128)(2,1)} %param.19) | copy-start | bytes 2359300
  48.0 16.9 %copy-start.3 = (f32[1,4,768]{2,1,0:T(4,128)S(1)}, f32[1,4,768]{2,1,0:T(4,128)}, u32[]{:S(2)}) copy-start(f32[1,4,768]{2,1,0:T(4,128)} %param.16) | copy-start | bytes 36868

commit v7 on v6

--- a/solution.py
+++ b/solution.py
@@ -171,7 +171,7 @@
     ranks = up_ref.shape[1]
     seg = own_segments(rows, lengths_ref)
     there = 1 - lax.axis_index("zl")
-    rank = mine_ref[:, quarter : quarter + HEAD] + other_ref[there, :, quarter : quarter + HEAD].astype(F32)
+    rank = mine_ref[:, quarter : quarter + HEAD].astype(F32) + other_ref[there, :, quarter : quarter + HEAD].astype(F32)
     rank = jnp.concatenate([rank] * (reqs * ranks // HEAD), axis=1)
     owner = lax.broadcasted_iota(jnp.int32, rank.shape, 1) // ranks
     rank = jnp.where(seg == owner, rank, 0.0).astype(BF16)
@@ -179,7 +179,7 @@
     gates = jnp.zeros((rows, quarter), F32)
     for r in range(reqs):
         gates = jnp.where(seg == r, gate_ref[r : r + 1, :], gates)
-    branch = mine_ref[:, 0:quarter] + other_ref[there, :, 0:quarter].astype(F32)
+    branch = mine_ref[:, 0:quarter].astype(F32) + other_ref[there, :, 0:quarter].astype(F32)
     branch = branch + jnp.dot(rank, ups, preferred_element_type=F32)
     out_ref[...] = (state_ref[...].astype(F32) + gates * branch).astype(out_ref.dtype)
 
@@ -252,7 +252,7 @@
         fold_kernel,
         in_specs=[vmem, vmem],
         out_specs=[vmem, vmem],
-        out_shape=[jax.ShapeDtypeStruct((rows, quarter + HEAD), F32), jax.ShapeDtypeStruct((rows, quarter + HEAD), BF16)],
+        out_shape=[jax.ShapeDtypeStruct((rows, quarter + HEAD), BF16)] * 2,
         compiler_params=params,
     )(keep, cores)
     other = lax.all_gather(other, "zl", axis=0, tiled=False)

time: 67.1 us -> 67.1 us (level)
  no operation moved by 1% of the time
where the time goes in v7:
time: 67.1 us; the launch traced here: 66.8 us
  blocking collectives  41.3 us (62%)
  starting transfers between devices  14 us (21%)
  Pallas kernels  8.83 us (13%)
  local copies, waits for them, and re-layouts  2.53 us (4%)
    all_gather x1, blocking collectives, shards(): kv = lax.all_gather(kv, 'yh', axis=0, tiled=True)  19.4 us
    all_gather x1, blocking collectives, shards(): cores = lax.all_gather(send, 'core', axis=0, tiled=False)  9.26 us
    all_gather x1, blocking collectives, shards(): other = lax.all_gather(other, 'zl', axis=0, tiled=False)  7.49 us
    ppermute x1, starting transfers between devices, shards(): lax.ppermute(stream[0], 'section', [(i, (i + 1) % sections) for i in rang...  5.5 us
    all_gather x1, blocking collectives, shards(): pair = lax.all_gather(query[0], 'yl', axis=0, tiled=True)  5.19 us
    all_to_all x1, starting transfers between devices, shards(): lax.all_to_all(parts, ('x', 'yl'), 0, 0, tiled=True, axis_index_groups=[O...  4.31 us
    all_to_all x1, starting transfers between devices, shards(): queries = lax.all_to_all(queries, 'x', 0, 0, tiled=True)  4.15 us
    pallas_call x1, Pallas kernels, shards(): pl.pallas_call(attend_kernel, in_specs=[smem, vmem, vmem], out_specs=hbm,...  3.74 us
  transfers between devices with their start and end apart: 3, of which 0 were waited for; matrix products, arithmetic and copies ran while one was open for 0% of the time, Pallas kernels for 3%

profile of v7, /device:TPU:1, one launch (start us, length us, event | category | flops | bytes accessed | tf_op | source)
XLA Modules:
  0.0 66.8 jit_solution(12168711721571098155)
XLA Ops:
  0.0 5.2 %all-gather = bf16[1,256,384]{2,1,0:T(8,128)(2,1)S(1)} all-gather(bf16[1,128,384]{2,1,0:T(8,128)(2,1)} %param.12), channel_id=2, replica_groups=mesh['section'=4,'x'=4,'yh'=4,'yl'=2,'zl'=2,'core'=2] {'yl'}, dimensions={1}, use_global_device_ids=true | all-gather | bytes 294912 | tf_op jit(solution)/shard_map/all_gather | solution.py:199
  5.2 0.9 %shard_map.100 = bf16[4,256,384]{2,1,0:T(8,128)(2,1)} custom-call(bf16[256,384]{1,0:T(8,128)(2,1)S(1)} %bitcast.19), custom_call_target="tpu_custom_call" | custom-call | tf_op jit(solution)/shard_map/pallas_call | solution.py:200
  6.2 4.1 %all-to-all-start = ((bf16[4,256,384]{2,1,0:T(8,128)(2,1)}), bf16[4,256,384]{2,1,0:T(8,128)(2,1)S(1)}, u32[]{:S(2)}, u32[]{:S(2)}) async-start(bf16[4,256,384]{2,1,0:T(8,128)(2,1)} %shard_map.100), calls=%async_computation | async-start | bytes 1572864 | tf_op jit(solution)/shard_map/all_to_all | solution.py:209
  10.3 0.0 copy-done.7
  10.3 19.4 %all_gather.19.kv_ref = bf16[512,768]{1,0:T(8,128)(2,1)S(1)} all-gather(bf16[128,768]{1,0:T(8,128)(2,1)S(1)} %pad_maximum_fusion), channel_id=1, replica_groups=mesh['section'=4,'x'=4,'yh'=4,'yl'=2,'zl'=2,'core'=2] {'yh'}, dimensions={0}, use_global_device_ids=true | all-gather | bytes 983040 | tf_op jit(solution)/shard_map/all_gather | solution.py:210
  29.7 0.0 all-to-all-done
  29.7 3.7 %shard_map.101 = bf16[8,400,128]{2,1,0:T(8,128)(2,1)} custom-call(s32[4]{0:T(128)S(1)} %copy-done.4, bf16[1024,384]{1,0:T(8,128)(2,1)S(1)} %bitcast.15, bf16[512,768]{1,0:T(8,128)(2,1)S(1)} %all_gather.19.kv_ref), custom_call_target="tpu_custom_call" | custom-call | tf_op jit(solution)/shard_map/pallas_call | solution.py:213
  33.5 4.3 %all-to-all-start.1 = ((bf16[8,400,128]{2,1,0:T(8,128)(2,1)}), bf16[8,400,128]{2,1,0:T(8,128)(2,1)S(1)}, u32[]{:S(2)}, u32[]{:S(2)}) async-start(bf16[8,400,128]{2,1,0:T(8,128)(2,1)} %shard_map.101), calls=%async_computation.1 | async-start | bytes 1638400 | tf_op jit(solution)/shard_map/all_to_all | solution.py:225
  37.8 5.5 %collective-permute-start = (bf16[128,768]{1,0:T(8,128)(2,1)}, bf16[128,768]{1,0:T(8,128)(2,1)}, u32[]{:S(2)}, u32[]{:S(2)}) collective-permute-start(bf16[128,768]{1,0:T(8,128)(2,1)} %bitcast.9), channel_id=1, source_target_pairs={{0,128},{128,256},{256,384},{384,0},{1,129},{129,257},{257,385},{3... | collective-permute-start | bytes 589832 | tf_op jit(solution)/shard_map/ppermute | solution.py:197
  43.3 0.0 copy-start
  43.3 1.7 %copy-done = bf16[1,384,3072]{2,1,0:T(8,128)(2,1)S(1)} copy-done((bf16[1,384,3072]{2,1,0:T(8,128)(2,1)S(1)}, bf16[1,384,3072]{2,1,0:T(8,128)(2,1)}, u32[]{:S(2)}) %copy-start) | copy-done | bytes 2359320
  44.9 0.2 shard_map.103.w_ref
  45.1 0.8 %copy-done.2 = bf16[1,8,384,64]{2,3,1,0:T(8,128)(2,1)S(1)} copy-done((bf16[1,8,384,64]{2,3,1,0:T(8,128)(2,1)S(1)}, bf16[1,8,384,64]{2,3,1,0:T(8,128)(2,1)}, u32[]{:S(2)}) %copy-start.2) | copy-done | bytes 393240
  45.9 0.0 copy-done.5
  45.9 0.6 shard_map.102.down_ref
  46.5 0.0 all-to-all-done.1.part_ref
  46.5 1.4 %shard_map.104 = (bf16[128,1664]{1,0:T(8,128)(2,1)S(1)}, bf16[128,1664]{1,0:T(8,128)(2,1)S(1)}) custom-call(s32[4]{0:T(128)S(1)} %copy-done.4, bf16[8,400,128]{2,1,0:T(8,128)(2,1)S(1)} %all-to-all-done.1.part_ref, bf16[4,64,384]{2,1,0:T(8,128)(2,1)S(1)} %shard_map.102.down_ref, bf16[384,3072]{1,0:T(8,128)(2,1)S(1)} %shard_map.103.w_ref), custom_call_target="tpu_custom_call" | custom-call | tf_op jit(solution)/shard_map/pallas_call | solution.py:243
  48.0 0.0 copy-start.1
  48.0 0.0 copy-start.3
  48.0 9.3 %all-gather.1 = bf16[256,1664]{1,0:T(8,128)(2,1)S(1)} all-gather(bf16[128,1664]{1,0:T(8,128)(2,1)S(1)} %get-tuple-element.10), channel_id=3, replica_groups=mesh['section'=4,'x'=4,'yh'=4,'yl'=2,'zl'=2,'core'=2] {'core'}, dimensions={0}, use_global_device_ids=true | all-gather | bytes 1277952 | tf_op jit(solution)/shard_map/all_gather | solution.py:250
  57.3 0.1 shard_map.105
  57.4 7.5 %all-gather.2 = bf16[256,896]{1,0:T(8,128)(2,1)S(1)} all-gather(bf16[128,896]{1,0:T(8,128)(2,1)S(1)} %get-tuple-element.12), channel_id=4, replica_groups=mesh['section'=4,'x'=4,'yh'=4,'yl'=2,'zl'=2,'core'=2] {'zl'}, dimensions={0}, use_global_device_ids=true | all-gather | bytes 688128 | tf_op jit(solution)/shard_map/all_gather | solution.py:258
  64.9 0.0 collective-permute-done.state_ref
  64.9 1.9 %shard_map.106 = bf16[128,768]{1,0:T(8,128)(2,1)} custom-call(s32[4]{0:T(128)S(1)} %copy-done.4, s32[4]{0:T(128)S(1)} %copy-done.5, bf16[128,896]{1,0:T(8,128)(2,1)S(1)} %get-tuple-element.11.mine_ref, bf16[2,128,896]{2,1,0:T(8,128)(2,1)S(1)} %bitcast.17, bf16[128,768]{1,0:T(8,128)(2,1)} %collective-permute-done.state_ref, f32[4,768]{1,0:T(4,128)S(1)} %bitcast.21, ...), custom_call_target="tpu_custom_call" | custom-call | tf_op jit(solution)/shard_map/pallas_call | solution.py:260
  (10 shorter events, 0.0 us)
Async XLA Ops:
  0.0 10.3 %copy-start.7 = (bf16[1,128,384]{2,1,0:T(8,128)(2,1)S(1)}, bf16[1,128,384]{2,1,0:T(8,128)(2,1)}, u32[]{:S(2)}) copy-start(bf16[1,128,384]{2,1,0:T(8,128)(2,1)} %param.13) | copy-start | bytes 294916
  0.0 10.3 %copy-start.6 = (bf16[1,128,384]{2,1,0:T(8,128)(2,1)S(1)}, bf16[1,128,384]{2,1,0:T(8,128)(2,1)}, u32[]{:S(2)}) copy-start(bf16[1,128,384]{2,1,0:T(8,128)(2,1)} %param.14) | copy-start | bytes 294916
  0.0 29.7 %copy-start.4 = (s32[4]{0:T(128)S(1)}, s32[4]{0:T(128)}, u32[]{:S(2)}) copy-start(s32[4]{0:T(128)} %lengths_ref.5) | copy-start | bytes 52
  6.2 23.5 %all-to-all-start = ((bf16[4,256,384]{2,1,0:T(8,128)(2,1)}), bf16[4,256,384]{2,1,0:T(8,128)(2,1)S(1)}, u32[]{:S(2)}, u32[]{:S(2)}) async-start(bf16[4,256,384]{2,1,0:T(8,128)(2,1)} %shard_map.100), calls=%async_computation | async-start | bytes 1572864 | tf_op jit(solution)/shard_map/all_to_all | solution.py:209
  33.5 13.1 %all-to-all-start.1 = ((bf16[8,400,128]{2,1,0:T(8,128)(2,1)}), bf16[8,400,128]{2,1,0:T(8,128)(2,1)S(1)}, u32[]{:S(2)}, u32[]{:S(2)}) async-start(bf16[8,400,128]{2,1,0:T(8,128)(2,1)} %shard_map.101), calls=%async_computation.1 | async-start | bytes 1638400 | tf_op jit(solution)/shard_map/all_to_all | solution.py:225
  37.8 27.1 %collective-permute-start = (bf16[128,768]{1,0:T(8,128)(2,1)}, bf16[128,768]{1,0:T(8,128)(2,1)}, u32[]{:S(2)}, u32[]{:S(2)}) collective-permute-start(bf16[128,768]{1,0:T(8,128)(2,1)} %bitcast.9), channel_id=1, source_target_pairs={{0,128},{128,256},{256,384},{384,0},{1,129},{129,257},{257,385},{3... | collective-permute-start | bytes 589832 | tf_op jit(solution)/shard_map/ppermute | solution.py:197
  43.3 1.7 %copy-start = (bf16[1,384,3072]{2,1,0:T(8,128)(2,1)S(1)}, bf16[1,384,3072]{2,1,0:T(8,128)(2,1)}, u32[]{:S(2)}) copy-start(bf16[1,384,3072]{2,1,0:T(8,128)(2,1)} %param.17) | copy-start | bytes 7077892
  44.9 1.0 %copy-start.2 = (bf16[1,8,384,64]{2,3,1,0:T(8,128)(2,1)S(1)}, bf16[1,8,384,64]{2,3,1,0:T(8,128)(2,1)}, u32[]{:S(2)}) copy-start(bf16[1,8,384,64]{2,3,1,0:T(8,128)(2,1)} %param.18) | copy-start | bytes 1179652
  44.9 1.0 %copy-start.5 = (s32[4]{0:T(128)S(1)}, s32[4]{0:T(128)}, u32[]{:S(2)}) copy-start(s32[4]{0:T(128)} %adapter_ref.3) | copy-start | bytes 52
  48.0 16.9 %copy-start.1 = (bf16[1,8,64,768]{3,2,1,0:T(8,128)(2,1)S(1)}, bf16[1,8,64,768]{3,2,1,0:T(8,128)(2,1)}, u32[]{:S(2)}) copy-start(bf16[1,8,64,768]{3,2,1,0:T(8,128)(2,1)} %param.19) | copy-start | bytes 2359300
  48.0 16.9 %copy-start.3 = (f32[1,4,768]{2,1,0:T(4,128)S(1)}, f32[1,4,768]{2,1,0:T(4,128)}, u32[]{:S(2)}) copy-start(f32[1,4,768]{2,1,0:T(4,128)} %param.16) | copy-start | bytes 36868

commit v8 on v4

--- a/solution.py
+++ b/solution.py
@@ -13,9 +13,10 @@
 NX, NYH, NYL = 4, 4, 2
 NZ, NC = 2, 2
 STAT_ROWS = 16
+ORDER = [0, 5, 1, 4, 2, 7, 3, 6]
 F32 = jnp.float32
 BF16 = jnp.bfloat16
-VMEM_LIMIT = 32 * 1024 * 1024
+VMEM_LIMIT = 16 * 1024 * 1024
 
 
 def segment_of(position, lengths_ref):
@@ -93,7 +94,7 @@
         part = jnp.dot(vt_ref[h * HEAD : (h + 1) * HEAD, :], weight.astype(BF16), preferred_element_type=F32)
         part = (part * (1.0 / total)).astype(BF16)
         for i in range(blocks):
-            out_ref[(i % NYL) * NX + i // NYL, h * HEAD : (h + 1) * HEAD, :] = part[:, i * rows : (i + 1) * rows]
+            out_ref[ORDER.index(i), h * HEAD : (h + 1) * HEAD, :] = part[:, i * rows : (i + 1) * rows]
         send(h * HEAD, HEAD)
         level = top * scale + jnp.log2(total)
         a = level.astype(BF16).astype(F32)
@@ -104,7 +105,7 @@
     blank = [jnp.zeros((1, n_q), F32)] * (STAT_ROWS - 3 * heads)
     stats = jnp.concatenate(high + mid + low + blank, axis=0).astype(BF16)
     for i in range(blocks):
-        out_ref[(i % NYL) * NX + i // NYL, feats : feats + STAT_ROWS, :] = stats[:, i * rows : (i + 1) * rows]
+        out_ref[ORDER.index(i), feats : feats + STAT_ROWS, :] = stats[:, i * rows : (i + 1) * rows]
     send(feats, STAT_ROWS)
     for copy in copies:
         copy.wait()
@@ -218,7 +219,7 @@
         ],
         compiler_params=params,
     )(lengths, queries.reshape(group * rows, feats), kv)
-    parts = lax.all_to_all(parts, ("yl", "x"), 0, 0, tiled=True)
+    parts = lax.all_to_all(parts, ("x", "yl"), 0, 0, tiled=True, axis_index_groups=[ORDER])
 
     down = jnp.swapaxes(adapter_down[0], 1, 2)
     matrix, down = pl.pallas_call(

time: 67.4 us -> 67.1 us (level)
  no operation moved by 1% of the time
where the time goes in v8:
time: 67.1 us; the launch traced here: 66.7 us
  blocking collectives  41.2 us (61%)
  starting transfers between devices  13.9 us (21%)
  Pallas kernels  8.8 us (13%)
  local copies, waits for them, and re-layouts  2.69 us (4%)
    all_gather x1, blocking collectives, shards(): kv = lax.all_gather(kv, 'yh', axis=0, tiled=True)  19.4 us
    all_gather x1, blocking collectives, shards(): cores = lax.all_gather(send, 'core', axis=0, tiled=False)  9.13 us
    all_gather x1, blocking collectives, shards(): other = lax.all_gather(other, 'zl', axis=0, tiled=False)  7.49 us
    ppermute x1, starting transfers between devices, shards(): lax.ppermute(stream[0], 'section', [(i, (i + 1) % sections) for i in rang...  5.48 us
    all_gather x1, blocking collectives, shards(): pair = lax.all_gather(query[0], 'yl', axis=0, tiled=True)  5.19 us
    all_to_all x1, starting transfers between devices, shards(): lax.all_to_all(parts, ('x', 'yl'), 0, 0, tiled=True, axis_index_groups=[O...  4.31 us
    all_to_all x1, starting transfers between devices, shards(): queries = lax.all_to_all(queries, 'x', 0, 0, tiled=True)  4.15 us
    pallas_call x1, Pallas kernels, shards(): pl.pallas_call(attend_kernel, in_specs=[smem, vmem, vmem], out_specs=hbm,...  3.73 us
  transfers between devices with their start and end apart: 3, of which 0 were waited for; matrix products, arithmetic and copies ran while one was open for 0% of the time, Pallas kernels for 3%

profile of v8, /device:TPU:1, one launch (start us, length us, event | category | flops | bytes accessed | tf_op | source)
XLA Modules:
  0.0 66.7 jit_solution(17710826627753856853)
XLA Ops:
  0.0 5.2 %all-gather = bf16[1,256,384]{2,1,0:T(8,128)(2,1)S(1)} all-gather(bf16[1,128,384]{2,1,0:T(8,128)(2,1)} %param.12), channel_id=2, replica_groups=mesh['section'=4,'x'=4,'yh'=4,'yl'=2,'zl'=2,'core'=2] {'yl'}, dimensions={1}, use_global_device_ids=true | all-gather | bytes 294912 | tf_op jit(solution)/shard_map/all_gather | solution.py:196
  5.2 0.9 %shard_map.100 = bf16[4,256,384]{2,1,0:T(8,128)(2,1)} custom-call(bf16[256,384]{1,0:T(8,128)(2,1)S(1)} %bitcast.19), custom_call_target="tpu_custom_call" | custom-call | tf_op jit(solution)/shard_map/pallas_call | solution.py:197
  6.2 4.1 %all-to-all-start = ((bf16[4,256,384]{2,1,0:T(8,128)(2,1)}), bf16[4,256,384]{2,1,0:T(8,128)(2,1)S(1)}, u32[]{:S(2)}, u32[]{:S(2)}) async-start(bf16[4,256,384]{2,1,0:T(8,128)(2,1)} %shard_map.100), calls=%async_computation | async-start | bytes 1572864 | tf_op jit(solution)/shard_map/all_to_all | solution.py:206
  10.3 0.0 copy-done.6
  10.3 0.0 copy-done.7
  10.3 0.0 copy-start.5
  10.3 19.4 %all_gather.19.kv_ref = bf16[512,768]{1,0:T(8,128)(2,1)S(1)} all-gather(bf16[128,768]{1,0:T(8,128)(2,1)S(1)} %pad_maximum_fusion), channel_id=1, replica_groups=mesh['section'=4,'x'=4,'yh'=4,'yl'=2,'zl'=2,'core'=2] {'yh'}, dimensions={0}, use_global_device_ids=true | all-gather | bytes 983040 | tf_op jit(solution)/shard_map/all_gather | solution.py:207
  29.7 0.0 all-to-all-done
  29.7 3.7 %shard_map.101 = bf16[8,400,128]{2,1,0:T(8,128)(2,1)} custom-call(s32[4]{0:T(128)S(1)} %copy-done.4, bf16[1024,384]{1,0:T(8,128)(2,1)S(1)} %bitcast.15, bf16[512,768]{1,0:T(8,128)(2,1)S(1)} %all_gather.19.kv_ref), custom_call_target="tpu_custom_call" | custom-call | tf_op jit(solution)/shard_map/pallas_call | solution.py:210
  33.5 4.3 %all-to-all-start.1 = ((bf16[8,400,128]{2,1,0:T(8,128)(2,1)}), bf16[8,400,128]{2,1,0:T(8,128)(2,1)S(1)}, u32[]{:S(2)}, u32[]{:S(2)}) async-start(bf16[8,400,128]{2,1,0:T(8,128)(2,1)} %shard_map.101), calls=%async_computation.1 | async-start | bytes 1638400 | tf_op jit(solution)/shard_map/all_to_all | solution.py:222
  37.8 5.5 %collective-permute-start = (bf16[128,768]{1,0:T(8,128)(2,1)}, bf16[128,768]{1,0:T(8,128)(2,1)}, u32[]{:S(2)}, u32[]{:S(2)}) collective-permute-start(bf16[128,768]{1,0:T(8,128)(2,1)} %bitcast.9), channel_id=1, source_target_pairs={{0,128},{128,256},{256,384},{384,0},{1,129},{129,257},{257,385},{3... | collective-permute-start | bytes 589832 | tf_op jit(solution)/shard_map/ppermute | solution.py:194
  43.3 0.0 copy-start
  43.3 1.7 %copy-done = bf16[1,384,3072]{2,1,0:T(8,128)(2,1)S(1)} copy-done((bf16[1,384,3072]{2,1,0:T(8,128)(2,1)S(1)}, bf16[1,384,3072]{2,1,0:T(8,128)(2,1)}, u32[]{:S(2)}) %copy-start) | copy-done | bytes 2359320
  44.9 1.0 %copy-done.2 = bf16[1,8,384,64]{2,3,1,0:T(8,128)(2,1)S(1)} copy-done((bf16[1,8,384,64]{2,3,1,0:T(8,128)(2,1)S(1)}, bf16[1,8,384,64]{2,3,1,0:T(8,128)(2,1)}, u32[]{:S(2)}) %copy-start.2) | copy-done | bytes 393240
  45.9 0.7 %shard_map.102 = (bf16[384,3072]{1,0:T(8,128)(2,1)S(1)}, bf16[4,64,384]{2,1,0:T(8,128)(2,1)S(1)}) custom-call(s32[4]{0:T(128)S(1)} %copy-done.5, bf16[384,3072]{1,0:T(8,128)(2,1)S(1)} %bitcast.16, bf16[8,64,384]{2,1,0:T(8,128)(2,1)S(1)} %bitcast.20), custom_call_target="tpu_custom_call" | custom-call | tf_op jit(solution)/shard_map/pallas_call | solution.py:225
  46.6 0.0 all-to-all-done.1.part_ref
  46.7 1.4 %shard_map.103 = (bf16[128,1664]{1,0:T(8,128)(2,1)S(1)}, f32[128,1664]{1,0:T(8,128)S(1)}) custom-call(s32[4]{0:T(128)S(1)} %copy-done.4, bf16[8,400,128]{2,1,0:T(8,128)(2,1)S(1)} %all-to-all-done.1.part_ref, bf16[4,64,384]{2,1,0:T(8,128)(2,1)S(1)} %get-tuple-element.11.down_ref, bf16[384,3072]{1,0:T(8,128)(2,1)S(1)} %get-tuple-element.12.w_ref), custom_call_target="tpu_custom_call" | custom-call | tf_op jit(solution)/shard_map/pallas_call | solution.py:236
  48.1 0.0 copy-start.1
  48.1 0.0 copy-start.3
  48.1 9.1 %all-gather.1 = bf16[256,1664]{1,0:T(8,128)(2,1)S(1)} all-gather(bf16[128,1664]{1,0:T(8,128)(2,1)S(1)} %get-tuple-element.14), channel_id=3, replica_groups=mesh['section'=4,'x'=4,'yh'=4,'yl'=2,'zl'=2,'core'=2] {'core'}, dimensions={0}, use_global_device_ids=true | all-gather | bytes 1277952 | tf_op jit(solution)/shard_map/all_gather | solution.py:243
  57.3 0.1 shard_map.104
  57.3 7.5 %all-gather.2 = bf16[256,896]{1,0:T(8,128)(2,1)S(1)} all-gather(bf16[128,896]{1,0:T(8,128)(2,1)S(1)} %get-tuple-element.16), channel_id=4, replica_groups=mesh['section'=4,'x'=4,'yh'=4,'yl'=2,'zl'=2,'core'=2] {'zl'}, dimensions={0}, use_global_device_ids=true | all-gather | bytes 688128 | tf_op jit(solution)/shard_map/all_gather | solution.py:251
  64.8 0.0 collective-permute-done.state_ref
  64.9 1.9 %shard_map.105 = bf16[128,768]{1,0:T(8,128)(2,1)} custom-call(s32[4]{0:T(128)S(1)} %copy-done.4, s32[4]{0:T(128)S(1)} %copy-done.5, f32[128,896]{1,0:T(8,128)S(1)} %get-tuple-element.15.mine_ref, bf16[2,128,896]{2,1,0:T(8,128)(2,1)S(1)} %bitcast.17, bf16[128,768]{1,0:T(8,128)(2,1)} %collective-permute-done.state_ref, f32[4,768]{1,0:T(4,128)S(1)} %bitcast.21, ...), custom_call_target="tpu_custom_call" | custom-call | tf_op jit(solution)/shard_map/pallas_call | solution.py:253
  (9 shorter events, 0.0 us)
Async XLA Ops:
  0.0 10.3 %copy-start.6 = (bf16[1,128,384]{2,1,0:T(8,128)(2,1)S(1)}, bf16[1,128,384]{2,1,0:T(8,128)(2,1)}, u32[]{:S(2)}) copy-start(bf16[1,128,384]{2,1,0:T(8,128)(2,1)} %param.14) | copy-start | bytes 294916
  0.0 10.3 %copy-start.7 = (bf16[1,128,384]{2,1,0:T(8,128)(2,1)S(1)}, bf16[1,128,384]{2,1,0:T(8,128)(2,1)}, u32[]{:S(2)}) copy-start(bf16[1,128,384]{2,1,0:T(8,128)(2,1)} %param.13) | copy-start | bytes 294916
  0.0 29.7 %copy-start.4 = (s32[4]{0:T(128)S(1)}, s32[4]{0:T(128)}, u32[]{:S(2)}) copy-start(s32[4]{0:T(128)} %lengths_ref.5) | copy-start | bytes 52
  6.2 23.6 %all-to-all-start = ((bf16[4,256,384]{2,1,0:T(8,128)(2,1)}), bf16[4,256,384]{2,1,0:T(8,128)(2,1)S(1)}, u32[]{:S(2)}, u32[]{:S(2)}) async-start(bf16[4,256,384]{2,1,0:T(8,128)(2,1)} %shard_map.100), calls=%async_computation | async-start | bytes 1572864 | tf_op jit(solution)/shard_map/all_to_all | solution.py:206
  10.3 32.9 %copy-start.5 = (s32[4]{0:T(128)S(1)}, s32[4]{0:T(128)}, u32[]{:S(2)}) copy-start(s32[4]{0:T(128)} %adapter_ref.3) | copy-start | bytes 52
  33.5 13.2 %all-to-all-start.1 = ((bf16[8,400,128]{2,1,0:T(8,128)(2,1)}), bf16[8,400,128]{2,1,0:T(8,128)(2,1)S(1)}, u32[]{:S(2)}, u32[]{:S(2)}) async-start(bf16[8,400,128]{2,1,0:T(8,128)(2,1)} %shard_map.101), calls=%async_computation.1 | async-start | bytes 1638400 | tf_op jit(solution)/shard_map/all_to_all | solution.py:222
  37.8 27.1 %collective-permute-start = (bf16[128,768]{1,0:T(8,128)(2,1)}, bf16[128,768]{1,0:T(8,128)(2,1)}, u32[]{:S(2)}, u32[]{:S(2)}) collective-permute-start(bf16[128,768]{1,0:T(8,128)(2,1)} %bitcast.9), channel_id=1, source_target_pairs={{0,128},{128,256},{256,384},{384,0},{1,129},{129,257},{257,385},{3... | collective-permute-start | bytes 589832 | tf_op jit(solution)/shard_map/ppermute | solution.py:194
  43.3 1.7 %copy-start = (bf16[1,384,3072]{2,1,0:T(8,128)(2,1)S(1)}, bf16[1,384,3072]{2,1,0:T(8,128)(2,1)}, u32[]{:S(2)}) copy-start(bf16[1,384,3072]{2,1,0:T(8,128)(2,1)} %param.17) | copy-start | bytes 7077892
  44.9 1.0 %copy-start.2 = (bf16[1,8,384,64]{2,3,1,0:T(8,128)(2,1)S(1)}, bf16[1,8,384,64]{2,3,1,0:T(8,128)(2,1)}, u32[]{:S(2)}) copy-start(bf16[1,8,384,64]{2,3,1,0:T(8,128)(2,1)} %param.18) | copy-start | bytes 1179652
  48.1 16.7 %copy-start.1 = (bf16[1,8,64,768]{3,2,1,0:T(8,128)(2,1)S(1)}, bf16[1,8,64,768]{3,2,1,0:T(8,128)(2,1)}, u32[]{:S(2)}) copy-start(bf16[1,8,64,768]{3,2,1,0:T(8,128)(2,1)} %param.19) | copy-start | bytes 2359300
  48.1 16.7 %copy-start.3 = (f32[1,4,768]{2,1,0:T(4,128)S(1)}, f32[1,4,768]{2,1,0:T(4,128)}, u32[]{:S(2)}) copy-start(f32[1,4,768]{2,1,0:T(4,128)} %param.16) | copy-start | bytes 36868
